TPU v7x, 256 devices: a whole 4x4x8 slice. The times are simulated.
256 devices in a mesh: dp: 2 (over x_lo), ctx: 8 (over y, x_hi), exp: 16 (over z, core).
Axes of the slice: x: 4 (x_hi: 2, x_lo: 2; x = x_hi * 2 + x_lo), y: 4, z: 8, core: 2. Of those that a mesh axis runs over, the one named last changes fastest.
Arguments:
- queries: bfloat16 [32768, 4096], P(('dp', 'ctx', 'exp')), may hold values from -64 to 64
- keys: bfloat16 [32768, 256], P(('dp', 'ctx', 'exp')), may hold values from -24 to 24
- values: bfloat16 [32768, 256], P(('dp', 'ctx', 'exp')), may hold values from -6 to 6
- lengths: int32 [2, 12], P('dp'), may hold values from 1 to 2048, 16384 in all within a row
- hidden: bfloat16 [32768, 4096], P(('dp', 'ctx', 'exp')), may hold values from -6 to 6
- norm_gain: float32 [4096], replicated, may hold values from 0.1 to 1.9
- routes: int32 [32768, 2], P(('dp', 'ctx', 'exp')), may hold values from 0 to 15, all different within a row; in each aligned block of 128 rows (0 to 127, 128 to 255, ...) at most 24 rows name the same one
- gates: float32 [32768, 2], P(('dp', 'ctx', 'exp')), may hold values from 0.2 to 1
- w_gate: bfloat16 [16, 4096, 768], P('exp', None, ('dp', 'ctx')), may hold values from -0.09375 to 0.09375
- w_up: bfloat16 [16, 4096, 768], P('exp', None, ('dp', 'ctx')), may hold values from -0.09375 to 0.09375
- w_down: bfloat16 [16, 4096, 768], P('exp', None, ('dp', 'ctx')), may hold values from -0.21875 to 0.21875
Outputs:
- context: bfloat16 [32768, 4096], P(('dp', 'ctx', 'exp'))
- expert_mix: bfloat16 [32768, 4096], P(('dp', 'ctx', 'exp'))
Inputs may be any that keep to these rules, and one draw needn't show every extreme that they name: `routes`: each row names 2 different experts. In the rows of one device (aligned blocks of 128 rows) no expert is named more than 24 times, a bound that some block reaches. `lengths`: each row sums to 16384; its longest rollout has exactly 2048 tokens.
All inputs are finite; a program needn't handle non-finite values.
Results may differ from a plain program's by a relative error of at most 0.014.
Values may be sent and summed in bfloat16 or wider, within the bound.
A program may use at most 192 MiB of HBM per device.

v0:
```python
import math

import jax
import jax.numpy as jnp
from jax import lax
from jax.sharding import PartitionSpec as P

HEAD_WIDTH = 128
QUERY_HEADS = 32
KEY_HEADS = 2
TOPK = 2


def shifted(block, axis, distance):
    devices = range(lax.axis_size(axis))
    route = [(i - distance, i) for i in devices if i - distance in devices]
    return lax.ppermute(block, axis, route)


def rollout_of(positions, bounds):
    return jnp.sum((positions[:, None] >= bounds[None, :]).astype(jnp.int32), axis=1)


def expert_terms(token_rows, pieces):
    gate_piece, up_piece, down_piece = pieces
    gate_part = jnp.dot(token_rows, gate_piece, preferred_element_type=jnp.float32)
    up_part = jnp.dot(token_rows, up_piece, preferred_element_type=jnp.float32)
    active = (jax.nn.silu(gate_part) * up_part).astype(jnp.bfloat16)
    return lax.dot_general(
        active, down_piece, (((1,), (1,)), ((), ())), preferred_element_type=jnp.float32
    )


def shards(queries, keys, values, lengths, hidden, norm_gain, routes, gates, w_gate, w_up, w_down):
    device_local_tokens = queries.shape[0]
    exp_count = lax.axis_size("exp")
    block_len = device_local_tokens * exp_count
    head_grouping = QUERY_HEADS // KEY_HEADS
    ctx_place = lax.axis_index("ctx")
    exp_place = lax.axis_index("exp")
    query_pos = (ctx_place * exp_count + exp_place) * device_local_tokens + jnp.arange(
        device_local_tokens, dtype=jnp.int32
    )
    bounds = jnp.cumsum(lengths[0])
    query_seg = rollout_of(query_pos, bounds)
    scaling = 1.0 / math.sqrt(HEAD_WIDTH)
    query_heads = queries.reshape(device_local_tokens, KEY_HEADS, head_grouping, HEAD_WIDTH)
    stacked_rows = jnp.stack((keys, values))
    earlier = shifted(stacked_rows, "ctx", 1)
    starting = (
        jnp.full((KEY_HEADS, head_grouping, device_local_tokens), -1e30, jnp.float32),
        jnp.zeros((KEY_HEADS, head_grouping, device_local_tokens), jnp.float32),
        jnp.zeros((KEY_HEADS, head_grouping, device_local_tokens, HEAD_WIDTH), jnp.float32),
    )
    own_piece = lax.all_gather(stacked_rows, "exp", axis=1, tiled=True)
    prior_piece = lax.all_gather(earlier, "exp", axis=1, tiled=True)
    segment_length = own_piece.shape[1]
    own_pos = ctx_place * block_len + jnp.arange(segment_length, dtype=jnp.int32)
    key_pos = jnp.concatenate((own_pos, own_pos - block_len))
    joined_rows = jnp.concatenate((own_piece, prior_piece), axis=1)
    key_seg = rollout_of(key_pos, bounds)
    visible = (
        (key_pos[None, :] <= query_pos[:, None])
        & (key_pos[None, :] >= 0)
        & (key_seg[None, :] == query_seg[:, None])
    )

    def update(current):
        run_max, run_sum, run_acc = current
        key_head_rows = joined_rows[0].reshape(2 * segment_length, KEY_HEADS, HEAD_WIDTH)
        value_head_rows = joined_rows[1].reshape(2 * segment_length, KEY_HEADS, HEAD_WIDTH)
        scores = (
            jnp.einsum(
                "tkgd,skd->kgts", query_heads, key_head_rows, preferred_element_type=jnp.float32
            )
            * scaling
        )
        scores = jnp.where(visible[None, None], scores, -1e30)
        new_max = jnp.maximum(run_max, jnp.max(scores, axis=-1))
        probs = jnp.where(visible[None, None], jnp.exp(scores - new_max[..., None]), 0.0)
        new_sum = jnp.sum(probs, axis=-1)
        new_acc = jnp.einsum(
            "kgts,skd->kgtd",
            probs.astype(jnp.bfloat16),
            value_head_rows,
            preferred_element_type=jnp.float32,
        )
        return (new_max, new_sum, new_acc)

    final_max, final_sum, final_acc = lax.cond(
        jnp.any(visible), update, lambda current: current, starting
    )
    context = (
        (final_acc / final_sum[..., None])
        .transpose(2, 0, 1, 3)
        .reshape(device_local_tokens, QUERY_HEADS * HEAD_WIDTH)
        .astype(jnp.bfloat16)
    )
    hidden_f = hidden.astype(jnp.float32)
    normed = (
        hidden_f
        * lax.rsqrt(jnp.mean(hidden_f * hidden_f, axis=-1, keepdims=True) + 1e-06)
        * norm_gain
    ).astype(jnp.bfloat16)
    model_width = normed.shape[1]
    capacity = 3 * device_local_tokens * TOPK // (2 * exp_count)
    flat_routes = routes.reshape(-1)
    route_hits = (flat_routes[:, None] == jnp.arange(exp_count, dtype=jnp.int32)[None, :]).astype(
        jnp.int32
    )
    route_ranks = jnp.sum((jnp.cumsum(route_hits, axis=0) - route_hits) * route_hits, axis=1)
    route_slots = flat_routes * capacity + route_ranks
    owner_tokens = jnp.arange(device_local_tokens * TOPK, dtype=jnp.int32) // TOPK
    members = (
        jnp.full((exp_count * capacity,), device_local_tokens, jnp.int32)
        .at[route_slots]
        .set(owner_tokens)
    )
    padded_rows = jnp.concatenate((normed, jnp.zeros((1, model_width), jnp.bfloat16)))
    outgoing = padded_rows[members].reshape(exp_count, capacity, model_width)
    arrived = lax.all_to_all(outgoing, "exp", split_axis=0, concat_axis=0, tiled=True)
    gathered_rows = arrived.reshape(exp_count * capacity, model_width)
    gate_shard = w_gate[0]
    up_shard = w_up[0]
    down_shard = w_down[0]
    expert_sums = expert_terms(
        gathered_rows,
        (
            lax.all_gather(gate_shard, ("dp", "ctx"), axis=1, tiled=True),
            lax.all_gather(up_shard, ("dp", "ctx"), axis=1, tiled=True),
            lax.all_gather(down_shard, ("dp", "ctx"), axis=1, tiled=True),
        ),
    )
    returned = lax.all_to_all(
        expert_sums.astype(jnp.bfloat16).reshape(exp_count, capacity, model_width),
        "exp",
        split_axis=0,
        concat_axis=0,
        tiled=True,
    )
    picked_rows = returned.reshape(exp_count * capacity, model_width)[route_slots].reshape(
        device_local_tokens, TOPK, model_width
    )
    expert_mix = jnp.sum(gates[:, :, None] * picked_rows.astype(jnp.float32), axis=1).astype(
        jnp.bfloat16
    )
    return (context, expert_mix)


def solution(mesh):
    return jax.shard_map(
        shards,
        mesh=mesh,
        in_specs=(
            P(("dp", "ctx", "exp"), None),
            P(("dp", "ctx", "exp"), None),
            P(("dp", "ctx", "exp"), None),
            P("dp", None),
            P(("dp", "ctx", "exp"), None),
            P(),
            P(("dp", "ctx", "exp"), None),
            P(("dp", "ctx", "exp"), None),
            P("exp", None, ("dp", "ctx")),
            P("exp", None, ("dp", "ctx")),
            P("exp", None, ("dp", "ctx")),
        ),
        out_specs=(P(("dp", "ctx", "exp"), None), P(("dp", "ctx", "exp"), None)),
        check_vma=False,
    )
```

profile of v0, /device:TPU:1, one launch (start us, length us, event | category | flops | bytes accessed | tf_op | source)
XLA Modules:
  0.0 731.4 jit_solution(17974418958188506583)
XLA Ops:
  16.5 4.0 gather_fusion
  20.5 10.1 %all-to-all-start = ((bf16[16,24,4096]{2,1,0:T(8,128)(2,1)}), bf16[16,24,4096]{2,1,0:T(8,128)(2,1)S(1)}, u32[]{:S(2)}, u32[]{:S(2)}) async-start(bf16[16,24,4096]{2,1,0:T(8,128)(2,1)} %bitcast.82), calls=%async_computation | async-start | bytes 6291456 | tf_op jit(solution)/shard_map/all_to_all | solution.py:121
  31.6 70.1 %all-to-all-done = bf16[16,24,4096]{2,1,0:T(8,128)(2,1)S(1)} async-done(((bf16[16,24,4096]{2,1,0:T(8,128)(2,1)}), bf16[16,24,4096]{2,1,0:T(8,128)(2,1)S(1)}, u32[]{:S(2)}, u32[]{:S(2)}) %all-to-all-start) | async-done | bytes 3145760 | tf_op jit(solution)/shard_map/all_to_all | solution.py:121
  101.7 71.6 %all-gather.13.cloned.1.call-done = bf16[1,4096,768]{1,2,0:T(8,128)(2,1)} async-done(((bf16[1,4096,48]{1,2,0:T(8,128)(2,1)}), bf16[1,4096,768]{1,2,0:T(8,128)(2,1)}) %all-gather.13.cloned.1.call-update) | async-done | bytes 6291472 | tf_op jit(solution)/shard_map/all_gather | solution.py:129
  173.3 6.5 fusion.15
  179.8 151.1 %all-gather.15.cloned.1.call-done = bf16[1,4096,768]{1,2,0:T(8,128)(2,1)} async-done(((bf16[1,4096,48]{1,2,0:T(8,128)(2,1)}), bf16[1,4096,768]{1,2,0:T(8,128)(2,1)}) %all-gather.15.cloned.1.call-update) | async-done | bytes 6291472 | tf_op jit(solution)/shard_map/all_gather | solution.py:130
  330.8 157.5 %all-gather.17.cloned.1.call-done = bf16[1,4096,768]{1,2,0:T(8,128)(2,1)} async-done(((bf16[1,4096,48]{1,2,0:T(8,128)(2,1)}), bf16[1,4096,768]{1,2,0:T(8,128)(2,1)}) %all-gather.17.cloned.1.call-update) | async-done | bytes 6291472 | tf_op jit(solution)/shard_map/all_gather | solution.py:131
  488.4 13.3 %fusion.17 = bf16[384,4096]{1,0:T(8,128)(2,1)} fusion(bf16[1,4096,768]{1,2,0:T(8,128)(2,1)} %all-gather.17.cloned.1.call-done, bf16[384,4096]{1,0:T(8,128)(2,1)S(1)} %bitcast.88, bf16[1,4096,768]{1,2,0:T(8,128)(2,1)} %all-gather.15.cloned.1.call-done, f32[384,768]{1,0:T(8,128)} %fusion.15), kind=kOutput, calls=%fused_computation.22 | convolution fusion | flops 4835180544 | bytes 20054016 | tf_op jit(solution)/shard_map/dot_general | solution.py:29
  501.7 7.3 all-to-all-start.1
  509.0 2.8 collective-permute-start
  511.9 2.5 collective-permute-done
  515.5 5.2 fusion.40
  521.4 29.8 %all-gather.9.cloned.1.call-done = bf16[2,2048,256]{1,2,0:T(8,128)(2,1)} async-done(((bf16[2,128,256]{1,2,0:T(8,128)(2,1)}), bf16[2,2048,256]{1,2,0:T(8,128)(2,1)}) %all-gather.9.cloned.1.call-update) | async-done | bytes 2097168 | tf_op jit(solution)/shard_map/all_gather | solution.py:55
  551.2 65.9 %all-gather.11.cloned.1.call-done = bf16[2,2048,256]{1,2,0:T(8,128)(2,1)} async-done(((bf16[2,128,256]{1,2,0:T(8,128)(2,1)}), bf16[2,2048,256]{1,2,0:T(8,128)(2,1)}) %all-gather.11.cloned.1.call-update) | async-done | bytes 2097168 | tf_op jit(solution)/shard_map/all_gather | solution.py:56
  617.1 2.8 pad_maximum_fusion
  619.9 82.7 %conditional.1 = (f32[2,16,128]{2,1,0:T(8,128)S(1)}, f32[2,16,128,128]{3,2,1,0:T(8,128)}) conditional(s32[]{:T(128)} %convert_element_type.51, () %tuple.16, (pred[128,4096]{0,1:T(8,128)(4,1)}, bf16[2,4096,256]{1,2,0:T(8,128)(2,1)S(1)}, bf16[128,4096]{1,0:T(8,128)(2,1)S(1)}) %tuple.35), branch_computations={%region_4.5_spmd, %region_5.8_spmd} | conditional | flops 8808034304 | bytes 220823568 | solution.py:90
  619.9 2.5 fusion.41
  623.7 26.6 %fusion = (f32[2,16,128]{2,1,0:T(8,128)S(1)}, f32[2,4096,128,16]{2,1,3,0:T(8,128)}) fusion(pred[128,4096]{0,1:T(8,128)(4,1)} %get-tuple-element.7, bf16[4096,2,128,1]{0,2,3,1:T(8,128)(2,1)} %bitcast.83, bf16[128,2,16,128]{3,2,1,0:T(8,128)(2,1)} %bitcast.84), kind=kOutput, calls=%fused_computation.5 | convolution fusion | flops 4345294848 | bytes 70795264 | tf_op jit(solution)/shard_map/cond/branch_1_fun/tkgd,skd->kgts/dot_general | solution.py:73
  650.2 30.5 %fusion.3 = f32[2,16,128,128]{3,2,1,0:T(8,128)} fusion(bf16[4096,2,128,1]{0,2,3,1:T(8,128)(2,1)} %bitcast.89, f32[2,4096,128,16]{2,1,3,0:T(8,128)} %get-tuple-element.23, f32[2,16,128]{2,1,0:T(8,128)S(1)} %broadcast_maximum_fusion, pred[128,4096]{0,1:T(8,128)(4,1)} %get-tuple-element.7), kind=kOutput, calls=%fused_computation.8 | convolution fusion | flops 4378853376 | bytes 71843840 | tf_op jit(solution)/shard_map/cond/branch_1_fun/kgts,skd->kgtd/dot_general | solution.py:82
  680.7 21.6 %fusion.2 = f32[2,16,128]{2,1,0:T(8,128)S(1)} fusion(f32[2,4096,128,16]{2,1,3,0:T(8,128)} %get-tuple-element.23, f32[2,16,128]{2,1,0:T(8,128)S(1)} %broadcast_maximum_fusion, pred[128,4096]{0,1:T(8,128)(4,1)} %get-tuple-element.7), kind=kLoop, calls=%fused_computation.7 | loop fusion | flops 83881984 | bytes 67665920 | tf_op jit(solution)/shard_map/cond/branch_1_fun/reduce_sum | solution.py:81
  702.6 2.0 fusion.29
  706.7 3.2 gather_fusion.1
  709.8 5.4 reshape.139
  715.3 9.6 %multiply_reduce_fusion = bf16[128,4096]{1,0:T(8,128)(2,1)} fusion(f32[128,2,4096]{2,1,0:T(2,128)} %reshape.139, f32[128,2]{1,0:T(8,128)S(1)} %copy.37), kind=kLoop, calls=%fused_computation.24 | loop fusion | flops 1572864 | bytes 5243904 | tf_op jit(solution)/shard_map/reduce_sum | solution.py:144
  (64 shorter events, 14.7 us)
Async XLA Ops:
  7.2 6.6 copy-start
  7.2 166.1 %all-gather.13.cloned.1.call-start = ((), (), s32[]{:S(2)}) async-start(), calls=%async_computation.4 | async-start | bytes 6684672 | tf_op jit(solution)/shard_map/all_gather | solution.py:129
  7.9 322.9 %all-gather.15.cloned.1.call-start = ((), (), s32[]{:S(2)}) async-start(), calls=%async_computation.5 | async-start | bytes 6684672 | tf_op jit(solution)/shard_map/all_gather | solution.py:130
  8.7 479.7 %all-gather.17.cloned.1.call-start = ((), (), s32[]{:S(2)}) async-start(), calls=%async_computation.6 | async-start | bytes 6684672 | tf_op jit(solution)/shard_map/all_gather | solution.py:131
  20.5 10.2 %copy-start.4 = (bf16[128,256]{1,0:T(8,128)(2,1)S(1)}, bf16[128,256]{1,0:T(8,128)(2,1)}, u32[]{:S(2)}) copy-start(bf16[128,256]{1,0:T(8,128)(2,1)} %param.14) | copy-start | bytes 196612
  20.5 10.3 %copy-start.5 = (bf16[128,256]{1,0:T(8,128)(2,1)S(1)}, bf16[128,256]{1,0:T(8,128)(2,1)}, u32[]{:S(2)}) copy-start(bf16[128,256]{1,0:T(8,128)(2,1)} %param.15) | copy-start | bytes 196612
  20.5 81.2 %all-to-all-start = ((bf16[16,24,4096]{2,1,0:T(8,128)(2,1)}), bf16[16,24,4096]{2,1,0:T(8,128)(2,1)S(1)}, u32[]{:S(2)}, u32[]{:S(2)}) async-start(bf16[16,24,4096]{2,1,0:T(8,128)(2,1)} %bitcast.82), calls=%async_computation | async-start | bytes 6291456 | tf_op jit(solution)/shard_map/all_to_all | solution.py:121
  30.6 520.6 %all-gather.9.cloned.1.call-start = ((), (), s32[]{:S(2)}) async-start(), calls=%async_computation.2 | async-start | bytes 2228224 | tf_op jit(solution)/shard_map/all_gather | solution.py:55
  501.7 7.3 %copy-start.2 = (bf16[2,128,256]{1,2,0:T(8,128)(2,1)S(1)}, bf16[2,128,256]{1,2,0:T(8,128)(2,1)}, u32[]{:S(2)}) copy-start(bf16[2,128,256]{1,2,0:T(8,128)(2,1)} %pad_maximum_fusion.1) | copy-start | bytes 393220
  501.7 13.3 %copy-start.7 = (s32[1,12]{1,0:T(1,128)S(1)}, s32[1,12]{1,0:T(1,128)}, u32[]{:S(2)}) copy-start(s32[1,12]{1,0:T(1,128)} %param.16) | copy-start | bytes 148
  501.7 19.6 %copy-start.6 = (f32[128,2]{0,1:T(2,128)S(1)}, f32[128,2]{0,1:T(2,128)}, u32[]{:S(2)}) copy-start(f32[128,2]{0,1:T(2,128)} %param.20) | copy-start | bytes 3076
  501.7 205.0 %all-to-all-start.1 = ((bf16[16,24,4096]{2,1,0:T(8,128)(2,1)}), bf16[16,24,4096]{2,1,0:T(8,128)(2,1)S(1)}, u32[]{:S(2)}, u32[]{:S(2)}) async-start(bf16[16,24,4096]{2,1,0:T(8,128)(2,1)} %bitcast.86), calls=%async_computation.1 | async-start | bytes 6291456 | tf_op jit(solution)/shard_map/all_to_all | solution.py:134
  509.0 108.1 %all-gather.11.cloned.1.call-start = ((), (), s32[]{:S(2)}) async-start(), calls=%async_computation.3 | async-start | bytes 2228224 | tf_op jit(solution)/shard_map/all_gather | solution.py:56
  509.0 5.3 collective-permute-start
  514.4 0.7 copy-start.3
  617.1 2.8 copy-start.1
Sparse Core Ops, SparseCore 0:
  9.8 163.4 all-gather.12
  175.1 155.6 all-gather.14
  332.6 155.6 all-gather.16
  490.5 60.6 all-gather.8
  552.8 64.2 all-gather.10
where the time goes:
time: 732 us; the launch traced here: 731 us
  waiting for transfers between devices  551 us (75%)
  matrix products  76.9 us (11%)
  other arithmetic  46.3 us (6%)
  local copies, waits for them, and re-layouts  22.5 us (3%)
  starting transfers between devices  20.4 us (3%)
  between operations  14.6 us (2%)
    all_gather x1, waiting for transfers between devices, shards(): lax.all_gather(down_shard, ('dp', 'ctx'), axis=1, tiled=True)  158 us
    all_gather x1, waiting for transfers between devices, shards(): lax.all_gather(up_shard, ('dp', 'ctx'), axis=1, tiled=True)  151 us
    all_gather x1, waiting for transfers between devices, shards(): lax.all_gather(gate_shard, ('dp', 'ctx'), axis=1, tiled=True)  71.6 us
    all_to_all x1, waiting for transfers between devices, shards(): lax.all_to_all(outgoing, 'exp', split_axis=0, concat_axis=0, tiled=True)  70.1 us
    all_gather x1, waiting for transfers between devices, shards(): prior_piece = lax.all_gather(earlier, 'exp', axis=1, tiled=True)  65.9 us
    dot_general x1, matrix products, update(): jnp.einsum('kgts,skd->kgtd', probs.astype(jnp.bfloat16), value_head_rows,...  30.5 us
    all_gather x1, waiting for transfers between devices, shards(): own_piece = lax.all_gather(stacked_rows, 'exp', axis=1, tiled=True)  29.8 us
    dot_general x1, matrix products, update(): jnp.einsum('tkgd,skd->kgts', query_heads, key_head_rows, preferred_elemen...  26.6 us
  transfers between devices with their start and end apart: 8, of which 7 were waited for; matrix products, arithmetic and copies ran while one was open for 17% of the time, Pallas kernels for 0%

commit v1 on v0

v1 whole, which is shorter than its diff:
```python
import functools
import math

import jax
import jax.numpy as jnp
from jax import lax
from jax.experimental import pallas as pl
from jax.experimental.pallas import tpu as pltpu
from jax.sharding import PartitionSpec as P

MESH = pl.DeviceIdType.MESH
HEAD_WIDTH = 128
QUERY_HEADS = 32
KEY_HEADS = 2
SIDE = 4
DEPTH = 8
QUARTERS = 4
CAP = 24


def place():
    dp, ctx, ex = lax.axis_index("dp"), lax.axis_index("ctx"), lax.axis_index("exp")
    return (ctx % 2) * 2 + dp, ctx // 2, ex // 2, ex % 2


def device_at(x, y, ex):
    return (x % 2, y * 2 + x // 2, ex)


def slot_hits(routes):
    experts, tokens = 16, routes.shape[1]
    ids = lax.broadcasted_iota(jnp.int32, (experts, tokens), 0)
    hits = ((ids == routes[0:1, :]) | (ids == routes[1:2, :])).astype(jnp.float32)
    earlier = (
        lax.broadcasted_iota(jnp.int32, (tokens, tokens), 0)
        < lax.broadcasted_iota(jnp.int32, (tokens, tokens), 1)
    ).astype(jnp.bfloat16)
    ranks = jnp.dot(hits.astype(jnp.bfloat16), earlier, preferred_element_type=jnp.float32)
    ranks = jnp.where(hits > 0, ranks, -1.0).astype(jnp.int32)
    wanted = lax.broadcasted_iota(jnp.int32, (experts, CAP, tokens), 1)
    return (ranks[:, None, :] == wanted).astype(jnp.float32)


def exchange_kernel(
    w_gate, w_up, w_down, keys, values, hidden, gain, routes,
    wall, arrived, window,
    hidden_rows, packed,
    local_sem, out_sem, in_sem, route_out, route_in, kv_out, kv_in,
):
    x, y, z, core = place()
    dp, ctx, ex = lax.axis_index("dp"), lax.axis_index("ctx"), lax.axis_index("exp")
    right, left = lax.rem(x + 1, SIDE), lax.rem(x + SIDE - 1, SIDE)
    above, below = lax.rem(y + 1, SIDE), lax.rem(y + SIDE - 1, SIDE)
    across, over = lax.rem(x + 2, SIDE), lax.rem(y + 2, SIDE)
    to_right, to_left = device_at(right, y, ex), device_at(left, y, ex)
    to_above, to_below = device_at(x, above, ex), device_at(x, below, ex)
    next_ctx, prior_ctx = lax.rem(ctx + 1, 8), lax.rem(ctx + 7, 8)
    sibling = z * 2 + 1 - core

    hidden_copy = pltpu.make_async_copy(hidden, hidden_rows, local_sem.at[14])
    hidden_copy.start()
    quarter = wall.shape[-1]
    mine = y * SIDE + x
    local = []
    for m, source in enumerate((w_gate, w_up, w_down)):
        for q in range(QUARTERS):
            copy = pltpu.make_async_copy(
                source.at[:, pl.ds(q * quarter, quarter)], wall.at[m, q, mine], local_sem.at[m * QUARTERS + q]
            )
            copy.start()
            local.append(copy)
    width = keys.shape[1]
    key_copy = pltpu.make_async_copy(keys, window.at[DEPTH, core, :, pl.ds(0, width)], local_sem.at[12])
    value_copy = pltpu.make_async_copy(values, window.at[DEPTH, core, :, pl.ds(width, width)], local_sem.at[13])
    key_copy.start()
    value_copy.start()

    barrier = pltpu.get_barrier_semaphore()
    for neighbour in (to_right, to_left, to_above, to_below):
        pl.semaphore_signal(barrier, inc=1, device_id=neighbour, device_id_type=MESH)
    for step in range(1, 16):
        pl.semaphore_signal(barrier, inc=1, device_id=(dp, ctx, lax.rem(ex + step, 16)), device_id_type=MESH)
    for plane in range(DEPTH):
        pl.semaphore_signal(barrier, inc=1, device_id=(dp, prior_ctx, plane * 2 + core), device_id_type=MESH)
    pl.semaphore_wait(barrier, 4 + 15 + DEPTH)

    sent = []
    counts = [0, 0, 0]

    def send(m, first, count, shard, target):
        part = wall.at[m, pl.ds(first, count), shard]
        copy = pltpu.make_async_remote_copy(
            src_ref=part, dst_ref=part,
            send_sem=out_sem.at[m, counts[m]], recv_sem=in_sem.at[m, shard, first],
            device_id=target, device_id_type=MESH,
        )
        counts[m] += 1
        copy.start()
        sent.append(copy)

    def landed(m, first, count, shard):
        part = wall.at[m, pl.ds(first, count), shard]
        pltpu.make_async_copy(part, part, in_sem.at[m, shard, first]).wait()

    def at(shard_x, shard_y):
        return shard_y * SIDE + shard_x

    for m in range(3):
        for copy in local[m * QUARTERS:(m + 1) * QUARTERS]:
            copy.wait()
        for target in (to_right, to_left, to_above, to_below):
            send(m, 0, 4, mine, target)

    key_copy.wait()
    value_copy.wait()
    kv_copies = []
    for step in range(DEPTH):
        plane = lax.rem(z + step, DEPTH)
        if step == 0:
            target_ctx = next_ctx
        else:
            target_ctx = lax.rem(ctx + (z + step) // DEPTH, 8)
        copy = pltpu.make_async_remote_copy(
            src_ref=window.at[DEPTH, core], dst_ref=window.at[(DEPTH - step) % DEPTH, core],
            send_sem=kv_out.at[step], recv_sem=kv_in.at[(DEPTH - step) % DEPTH],
            device_id=(dp, target_ctx, plane * 2 + core), device_id_type=MESH,
        )
        copy.start()
        kv_copies.append(copy)

    hidden_copy.wait()
    picks = slot_hits(routes[...]).reshape(16 * CAP, -1).astype(jnp.bfloat16)
    rows = hidden_rows[...].astype(jnp.float32)
    scale = lax.rsqrt(jnp.mean(rows * rows, axis=-1, keepdims=True) + 1e-06)
    for q in range(QUARTERS):
        cols = pl.ds(q * quarter, quarter)
        normed = (hidden_rows[:, cols].astype(jnp.float32) * scale * gain[:, cols]).astype(jnp.bfloat16)
        block = jnp.dot(picks, normed, preferred_element_type=jnp.float32).astype(jnp.bfloat16)
        packed[:, :, cols] = block.reshape(16, CAP, quarter)
    own_rows = pltpu.make_async_copy(packed.at[ex], arrived.at[ex], local_sem.at[15])
    own_rows.start()
    route_copies = []
    for step in (8, 7, 9, 6, 10, 5, 11, 4, 12, 3, 13, 2, 14, 1, 15):
        peer = lax.rem(ex + step, 16)
        copy = pltpu.make_async_remote_copy(
            src_ref=packed.at[peer], dst_ref=arrived.at[ex],
            send_sem=route_out.at[step - 1], recv_sem=route_in.at[ex],
            device_id=(dp, ctx, peer), device_id_type=MESH,
        )
        copy.start()
        route_copies.append(copy)

    for m in range(3):
        landed(m, 0, 4, at(left, y))
        send(m, 0, 2, at(left, y), to_right)
        send(m, 1, 2, at(left, y), to_above)
        send(m, 1, 2, at(left, y), to_below)
        landed(m, 0, 4, at(right, y))
        send(m, 2, 2, at(right, y), to_left)
        send(m, 1, 2, at(right, y), to_above)
        send(m, 1, 2, at(right, y), to_below)
        landed(m, 0, 4, at(x, below))
        send(m, 0, 2, at(x, below), to_above)
        for q in (0, 3):
            send(m, q, 1, at(x, below), to_right)
            send(m, q, 1, at(x, below), to_left)
        landed(m, 0, 4, at(x, above))
        send(m, 2, 2, at(x, above), to_below)
        for q in (0, 3):
            send(m, q, 1, at(x, above), to_right)
            send(m, q, 1, at(x, above), to_left)

    for m in range(3):
        landed(m, 0, 2, at(across, y))
        send(m, 1, 1, at(across, y), to_above)
        send(m, 1, 1, at(across, y), to_below)
        landed(m, 2, 2, at(across, y))
        send(m, 2, 1, at(across, y), to_above)
        send(m, 2, 1, at(across, y), to_below)
        landed(m, 0, 2, at(x, over))
        send(m, 0, 1, at(x, over), to_right)
        send(m, 0, 1, at(x, over), to_left)
        landed(m, 2, 2, at(x, over))
        send(m, 3, 1, at(x, over), to_right)
        send(m, 3, 1, at(x, over), to_left)
        for side in (left, right):
            landed(m, 1, 2, at(side, below))
            send(m, 1, 1, at(side, below), to_above)
            landed(m, 1, 2, at(side, above))
            send(m, 2, 1, at(side, above), to_below)
        for side in (below, above):
            landed(m, 0, 1, at(left, side))
            landed(m, 3, 1, at(left, side))
            send(m, 0, 1, at(left, side), to_right)
            landed(m, 0, 1, at(right, side))
            landed(m, 3, 1, at(right, side))
            send(m, 3, 1, at(right, side), to_left)

    for slot in range(DEPTH):
        pltpu.make_async_copy(window.at[slot, core], window.at[slot, core], kv_in.at[slot]).wait()
    share = pltpu.make_async_remote_copy(
        src_ref=window.at[:, core], dst_ref=window.at[:, core],
        send_sem=kv_out.at[DEPTH], recv_sem=kv_in.at[DEPTH],
        device_id=(dp, ctx, sibling), device_id_type=MESH,
    )
    share.start()

    for m in range(3):
        landed(m, 1, 1, at(across, below))
        landed(m, 2, 1, at(across, below))
        send(m, 1, 1, at(across, below), to_above)
        landed(m, 1, 1, at(across, above))
        landed(m, 2, 1, at(across, above))
        send(m, 2, 1, at(across, above), to_below)
        landed(m, 0, 1, at(left, over))
        landed(m, 3, 1, at(left, over))
        send(m, 0, 1, at(left, over), to_right)
        landed(m, 0, 1, at(right, over))
        landed(m, 3, 1, at(right, over))
        send(m, 3, 1, at(right, over), to_left)

    own_rows.wait()
    for step in range(1, 16):
        peer = lax.rem(ex + step, 16)
        pltpu.make_async_copy(arrived.at[peer], arrived.at[peer], route_in.at[peer]).wait()
    for m in range(3):
        for side in (left, right):
            landed(m, 1, 1, at(side, over))
            landed(m, 2, 1, at(side, over))
        for side in (below, above):
            landed(m, 0, 1, at(across, side))
            landed(m, 3, 1, at(across, side))
        for q in range(QUARTERS):
            landed(m, q, 1, at(across, over))
    pltpu.make_async_copy(window.at[:, 1 - core], window.at[:, 1 - core], kv_in.at[DEPTH]).wait()
    share.wait_send()
    for copy in kv_copies + route_copies + sent:
        copy.wait_send()


def exchange(w_gate, w_up, w_down, keys, values, hidden, gain, routes):
    tokens, width = hidden.shape
    piece = w_gate.shape[0]
    anywhere, vmem = pl.BlockSpec(memory_space=pl.ANY), pl.BlockSpec(memory_space=pltpu.VMEM)
    bf16, dma = jnp.bfloat16, pltpu.SemaphoreType.DMA
    return pl.pallas_call(
        exchange_kernel,
        out_shape=(
            jax.ShapeDtypeStruct((3, QUARTERS, SIDE * SIDE, piece, width // QUARTERS), bf16),
            jax.ShapeDtypeStruct((16, CAP, width), bf16),
            jax.ShapeDtypeStruct((DEPTH + 1, 2, tokens, 2 * keys.shape[1]), bf16),
        ),
        in_specs=[anywhere] * 6 + [vmem] * 2,
        out_specs=[anywhere] * 3,
        scratch_shapes=[
            pltpu.VMEM((tokens, width), bf16),
            pltpu.VMEM((16, CAP, width), bf16),
            dma((16,)), dma((3, 40)), dma((3, 16, 4)), dma((15,)), dma((16,)), dma((9,)), dma((9,)),
        ],
        compiler_params=pltpu.CompilerParams(
            collective_id=0, has_side_effects=True, vmem_limit_bytes=40 * 1024 * 1024
        ),
        cost_estimate=pl.CostEstimate(flops=10**9, bytes_accessed=40 * 10**6, transcendentals=0),
        name="exchange",
    )(w_gate, w_up, w_down, keys, values, hidden, gain, routes)


def expert_kernel(rows, gate, up, down, out, gate_sum, up_sum, active):
    i = pl.program_id(0)
    turned = (((1,), (1,)), ((), ()))

    @pl.when(i == 0)
    def _():
        gate_sum[...] = jnp.zeros_like(gate_sum)
        up_sum[...] = jnp.zeros_like(up_sum)

    @pl.when(i < QUARTERS)
    def _():
        gate_sum[...] += lax.dot_general(rows[...], gate[0, 0], turned, preferred_element_type=jnp.float32)
        up_sum[...] += lax.dot_general(rows[...], up[0, 0], turned, preferred_element_type=jnp.float32)

    @pl.when(i == QUARTERS - 1)
    def _():
        g = gate_sum[...]
        active[...] = (g / (1.0 + jnp.exp(-g)) * up_sum[...]).astype(jnp.bfloat16)

    @pl.when(i >= QUARTERS)
    def _():
        out[...] = jnp.dot(active[...], down[0, 0], preferred_element_type=jnp.float32).astype(out.dtype)


def expert_block(rows, wall):
    count, width = rows.shape
    units, quarter = wall.shape[2], wall.shape[3]
    early = lambda i: jnp.minimum(i, QUARTERS - 1)
    late = lambda i: jnp.maximum(i - QUARTERS, 0)
    block = (1, 1, units, quarter)
    return pl.pallas_call(
        expert_kernel,
        grid=(2 * QUARTERS,),
        out_shape=jax.ShapeDtypeStruct((count, width), jnp.bfloat16),
        in_specs=[
            pl.BlockSpec((count, quarter), lambda i: (0, early(i))),
            pl.BlockSpec(block, lambda i: (0, early(i), 0, 0)),
            pl.BlockSpec(block, lambda i: (1, early(i), 0, 0)),
            pl.BlockSpec(block, lambda i: (2, late(i), 0, 0)),
        ],
        out_specs=pl.BlockSpec((count, quarter), lambda i: (0, late(i))),
        scratch_shapes=[
            pltpu.VMEM((count, units), jnp.float32),
            pltpu.VMEM((count, units), jnp.float32),
            pltpu.VMEM((count, units), jnp.bfloat16),
        ],
        compiler_params=pltpu.CompilerParams(vmem_limit_bytes=40 * 1024 * 1024),
        cost_estimate=pl.CostEstimate(flops=7 * 10**9, bytes_accessed=25 * 10**6, transcendentals=0),
        name="experts",
    )(rows, wall, wall, wall)


HEADS_AT_ONCE = 4


def attention_kernel(lengths, queries, window, out, bias):
    i = pl.program_id(0)
    tokens, keys = queries.shape[0], window.shape[0]
    ctx, ex = lax.axis_index("ctx"), lax.axis_index("exp")

    @pl.when(i == 0)
    def _():
        query_pos = (ctx * 16 + ex) * tokens + lax.broadcasted_iota(jnp.int32, (tokens, 1), 0)
        begin = jnp.zeros_like(query_pos)
        bound = jnp.int32(0)
        for r in range(lengths.shape[1]):
            bound = bound + lengths[0, r]
            begin = jnp.where(query_pos >= bound, bound, begin)
        step = 256
        for c in range(keys // step):
            key_pos = (
                ctx * 16 + (ex // 2) * 2 - 16
            ) * tokens + c * step + lax.broadcasted_iota(jnp.int32, (tokens, step), 1)
            seen = (key_pos <= query_pos) & (key_pos >= begin)
            bias[:, c * step:(c + 1) * step] = jnp.where(seen, 0.0, -1e30)

    group = i // (QUERY_HEADS // KEY_HEADS // HEADS_AT_ONCE)
    key_col = pl.multiple_of(group * HEAD_WIDTH, HEAD_WIDTH)
    value_col = pl.multiple_of((KEY_HEADS + group) * HEAD_WIDTH, HEAD_WIDTH)
    key_rows = window[:, pl.ds(key_col, HEAD_WIDTH)]
    value_rows = window[:, pl.ds(value_col, HEAD_WIDTH)]
    stacked = jnp.concatenate(
        [queries[:, h * HEAD_WIDTH:(h + 1) * HEAD_WIDTH] for h in range(HEADS_AT_ONCE)], axis=0
    )
    scores = lax.dot_general(stacked, key_rows, (((1,), (1,)), ((), ())), preferred_element_type=jnp.float32)
    scores = scores.reshape(HEADS_AT_ONCE, tokens, keys) + bias[...][None]
    top = jnp.max(scores, axis=-1, keepdims=True)
    probs = jnp.exp2((scores - top) * (math.log2(math.e) / math.sqrt(HEAD_WIDTH)))
    total = jnp.sum(probs, axis=-1, keepdims=True)
    summed = jnp.dot(
        probs.reshape(HEADS_AT_ONCE * tokens, keys).astype(jnp.bfloat16), value_rows,
        preferred_element_type=jnp.float32,
    ).reshape(HEADS_AT_ONCE, tokens, HEAD_WIDTH)
    result = (summed / total).astype(out.dtype)
    for h in range(HEADS_AT_ONCE):
        out[:, h * HEAD_WIDTH:(h + 1) * HEAD_WIDTH] = result[h]


def attend(lengths, queries, window):
    tokens, width = queries.shape
    columns = HEADS_AT_ONCE * HEAD_WIDTH
    return pl.pallas_call(
        attention_kernel,
        grid=(width // columns,),
        out_shape=jax.ShapeDtypeStruct((tokens, width), jnp.bfloat16),
        in_specs=[
            pl.BlockSpec(memory_space=pltpu.SMEM),
            pl.BlockSpec((tokens, columns), lambda i: (0, i)),
            pl.BlockSpec(window.shape, lambda i: (0, 0)),
        ],
        out_specs=pl.BlockSpec((tokens, columns), lambda i: (0, i)),
        scratch_shapes=[pltpu.VMEM((tokens, window.shape[0]), jnp.float32)],
        compiler_params=pltpu.CompilerParams(vmem_limit_bytes=40 * 1024 * 1024),
        cost_estimate=pl.CostEstimate(
            flops=20 * 10**9, bytes_accessed=10 * 10**6, transcendentals=10**7
        ),
        name="attention",
    )(lengths, queries, window)


def mix_kernel(routes, gates, returned, out):
    experts, tokens = 16, routes.shape[1]
    ids = lax.broadcasted_iota(jnp.int32, (experts, tokens), 0)
    weight = jnp.where(ids == routes[0:1, :], gates[0:1, :], 0.0)
    weight = weight + jnp.where(ids == routes[1:2, :], gates[1:2, :], 0.0)
    spread = (slot_hits(routes[...]) * weight[:, None, :]).reshape(experts * CAP, tokens)
    high = spread.astype(jnp.bfloat16)
    low = (spread - high.astype(jnp.float32)).astype(jnp.bfloat16)
    across = (((0,), (0,)), ((), ()))
    rows = returned[...]
    total = lax.dot_general(high, rows, across, preferred_element_type=jnp.float32)
    total = total + lax.dot_general(low, rows, across, preferred_element_type=jnp.float32)
    out[...] = total.astype(out.dtype)


def mix(routes, gates, returned):
    count, width = returned.shape
    tokens, quarter = routes.shape[1], width // QUARTERS
    return pl.pallas_call(
        mix_kernel,
        grid=(QUARTERS,),
        out_shape=jax.ShapeDtypeStruct((tokens, width), jnp.bfloat16),
        in_specs=[
            pl.BlockSpec((2, tokens), lambda i: (0, 0)),
            pl.BlockSpec((2, tokens), lambda i: (0, 0)),
            pl.BlockSpec((count, quarter), lambda i: (0, i)),
        ],
        out_specs=pl.BlockSpec((tokens, quarter), lambda i: (0, i)),
        compiler_params=pltpu.CompilerParams(vmem_limit_bytes=32 * 1024 * 1024),
        cost_estimate=pl.CostEstimate(flops=10**9, bytes_accessed=4 * 10**6, transcendentals=0),
        name="mix",
    )(routes, gates, returned)


def shards(queries, keys, values, lengths, hidden, norm_gain, routes, gates, w_gate, w_up, w_down):
    width = hidden.shape[1]
    turned = [jnp.swapaxes(w[0], 0, 1) for w in (w_gate, w_up, w_down)]
    wall, arrived, window = exchange(*turned, keys, values, hidden, norm_gain[None, :], routes.T)
    units = SIDE * SIDE * turned[0].shape[0]
    results = expert_block(arrived.reshape(16 * CAP, width), wall.reshape(3, QUARTERS, units, width // QUARTERS))
    returned = lax.all_to_all(results.reshape(16, CAP, width), "exp", split_axis=0, concat_axis=0, tiled=True)
    context = attend(lengths, queries, window.reshape(-1, window.shape[-1]))
    expert_mix = mix(routes.T, gates.T, returned.reshape(16 * CAP, width))
    return context, expert_mix


def solution(mesh):
    whole = P(("dp", "ctx", "exp"), None)
    weights = P("exp", None, ("dp", "ctx"))
    return jax.shard_map(
        shards,
        mesh=mesh,
        in_specs=(whole, whole, whole, P("dp", None), whole, P(), whole, whole, weights, weights, weights),
        out_specs=(whole, whole),
        check_vma=False,
    )
```

time: 732 us -> 240 us (0.33)
  waiting for transfers between devices: 551 us -> 39 us
  Pallas kernels: 0 us -> 182 us
  matrix products: 76.9 us -> 0 us
  other arithmetic: 46.3 us -> 0 us
  starting transfers between devices: 20.4 us -> 4.55 us
  between operations: 14.6 us -> 0.7 us
  local copies, waits for them, and re-layouts: 22.5 us -> 13.2 us
    all_gather x5 -> x0, waiting for transfers between devices: 476 us -> none  [the longest x1 158 us: shards(): lax.all_gather(down_shard, ('dp', 'ctx'), axis=1, tiled=True)]
    pallas_call x0 -> x4, Pallas kernels: none -> 182 us  [the longest x1 135 us: exchange(): pl.pallas_call(exchange_kernel, out_shape=(jax.ShapeDtypeStruct((3, QUART...]
    dot_general x4 -> x0, matrix products: 76.9 us -> none  [the longest x1 30.5 us: update(): jnp.einsum('kgts,skd->kgtd', probs.astype(jnp.bfloat16), value_head_rows,...]
    reduce_sum x6 -> x0, other arithmetic: 33.1 us -> none  [the longest x1 21.6 us: update(): new_sum = jnp.sum(probs, axis=-1)]
    all_to_all x2 -> x1, waiting for transfers between devices: 70.1 us -> 39 us  [shards(): lax.all_to_all(results.reshape(16, CAP, width), 'exp', split_axis=0, conc...]
    all_to_all x2 -> x1, starting transfers between devices: 17.4 us -> 4.55 us  [shards(): lax.all_to_all(results.reshape(16, CAP, width), 'exp', split_axis=0, conc...]
    unnamed x21 -> x30, local copies, waits for them, and re-layouts: 3.21 us -> 13.2 us
  transfers between devices with their start and end apart: 8 -> 1, of which waited for: 7 -> 1; matrix products, arithmetic and copies ran while one was open for 17% -> 0% of each run, Pallas kernels for 0% -> 12%
where the time goes in v1:
time: 240 us; the launch traced here: 239 us
  Pallas kernels  182 us (76%)
  waiting for transfers between devices  39 us (16%)
  local copies, waits for them, and re-layouts  13.2 us (6%)
  starting transfers between devices  4.55 us (2%)
    pallas_call x1, Pallas kernels, exchange(): pl.pallas_call(exchange_kernel, out_shape=(jax.ShapeDtypeStruct((3, QUART...  135 us
    all_to_all x1, waiting for transfers between devices, shards(): lax.all_to_all(results.reshape(16, CAP, width), 'exp', split_axis=0, conc...  39 us
    pallas_call x1, Pallas kernels, attend(): pl.pallas_call(attention_kernel, grid=(width // columns,), out_shape=jax....  29.1 us
    pallas_call x1, Pallas kernels, expert_block(): pl.pallas_call(expert_kernel, grid=(2 * QUARTERS,), out_shape=jax.ShapeDt...  13.9 us
    unnamed x30, local copies, waits for them, and re-layouts  13.2 us
  transfers between devices with their start and end apart: 1, of which 1 were waited for; matrix products, arithmetic and copies ran while one was open for 0% of the time, Pallas kernels for 12%

profile of v1, /device:TPU:1, one launch (start us, length us, event | category | flops | bytes accessed | tf_op | source)
XLA Modules:
  0.0 239.3 jit_solution(18303644748626089646)
XLA Ops:
  0.6 0.0 copy-start.1
  0.6 0.7 copy-done.1
  1.3 1.2 copy-done.4
  2.5 1.0 copy-done.6
  3.5 1.0 copy-done.7
  4.5 1.0 copy-done.8
  5.5 0.8 copy-done.9
  6.4 0.8 copy-done.10
  7.2 0.7 copy-done.11
  7.9 135.3 %exchange.1 = (bf16[3,4,16,48,1024]{4,3,2,1,0:T(8,128)(2,1)}, bf16[16,24,4096]{2,1,0:T(8,128)(2,1)S(1)}, bf16[9,2,128,512]{3,2,1,0:T(8,128)(2,1)S(1)}) custom-call(bf16[48,4096]{1,0:T(8,128)(2,1)S(1)} %bitcast.23, bf16[48,4096]{1,0:T(8,128)(2,1)S(1)} %bitcast.24, bf16[48,4096]{1,0:T(8,128)(2,1)S(1)} %bitcast.25, bf16[128,256]{1,0:T(8,128)(2,1)S(1)} %copy-done.9, ...), custom_call_target="tpu_custom_call" | custom-call | flops 1000000000 | bytes 40000000 | tf_op jit(solution)/shard_map/exchange/pallas_call | solution.py:246
  143.2 0.0 copy-start.13
  143.2 1.4 copy-done.13
  144.6 13.9 %experts.1 = bf16[384,4096]{1,0:T(8,128)(2,1)S(1)} custom-call(bf16[384,4096]{1,0:T(8,128)(2,1)S(1)} %bitcast.19, bf16[3,4,768,1024]{3,2,1,0:T(8,128)(2,1)} %bitcast.28, bf16[3,4,768,1024]{3,2,1,0:T(8,128)(2,1)} %bitcast.29, bf16[3,4,768,1024]{3,2,1,0:T(8,128)(2,1)} %bitcast.30), custom_call_target="tpu_custom_call" | custom-call | flops 7000000000 | bytes 25000000 | tf_op jit(solution)/shard_map/experts/pallas_call | solution.py:298
  158.5 0.0 copy-start
  158.5 1.6 copy-done
  160.2 4.6 %all-to-all-start = ((bf16[16,24,4096]{2,1,0:T(8,128)(2,1)}), bf16[16,24,4096]{2,1,0:T(8,128)(2,1)S(1)}, u32[]{:S(2)}, u32[]{:S(2)}) async-start(bf16[16,24,4096]{2,1,0:T(8,128)(2,1)} %bitcast.18), calls=%async_computation | async-start | bytes 6291456 | tf_op jit(solution)/shard_map/all_to_all | solution.py:428
  164.7 0.0 copy-done.12
  164.7 0.0 copy-start.5
  164.8 1.2 copy-done.5
  166.0 1.7 copy-done.14
  167.6 29.1 %attention.1 = bf16[128,4096]{1,0:T(8,128)(2,1)} custom-call(s32[1,12]{1,0:T(1,128)S(1)} %copy-done.12, bf16[128,4096]{1,0:T(8,128)(2,1)S(1)} %copy-done.5, bf16[2304,512]{1,0:T(8,128)(2,1)S(1)} %bitcast.27), custom_call_target="tpu_custom_call" | custom-call | flops 20000000000 | bytes 10000000 | tf_op jit(solution)/shard_map/attention/pallas_call | solution.py:369
  196.8 39.0 %all-to-all-done = bf16[16,24,4096]{2,1,0:T(8,128)(2,1)S(1)} async-done(((bf16[16,24,4096]{2,1,0:T(8,128)(2,1)}), bf16[16,24,4096]{2,1,0:T(8,128)(2,1)S(1)}, u32[]{:S(2)}, u32[]{:S(2)}) %all-to-all-start) | async-done | bytes 3145760 | tf_op jit(solution)/shard_map/all_to_all | solution.py:428
  235.8 0.0 copy-done.3
  235.8 3.5 %mix.1 = bf16[128,4096]{1,0:T(8,128)(2,1)} custom-call(s32[2,128]{1,0:T(2,128)S(1)} %bitcast.21, f32[2,128]{1,0:T(2,128)S(1)} %bitcast.22, bf16[384,4096]{1,0:T(8,128)(2,1)S(1)} %bitcast.17), custom_call_target="tpu_custom_call" | custom-call | flops 1000000000 | bytes 4000000 | tf_op jit(solution)/shard_map/mix/pallas_call | solution.py:406
  (12 shorter events, 0.0 us)
Async XLA Ops:
  0.6 0.7 copy-start.1
  1.3 1.2 copy-start.4
  2.5 1.0 copy-start.6
  3.5 1.0 copy-start.7
  4.5 1.0 copy-start.8
  5.5 0.8 copy-start.9
  6.4 0.8 copy-start.10
  7.2 0.7 copy-start.11
  143.2 1.4 copy-start.13
  158.5 1.7 copy-start
  160.2 4.6 %copy-start.12 = (s32[1,12]{1,0:T(1,128)S(1)}, s32[1,12]{1,0:T(1,128)}, u32[]{:S(2)}) copy-start(s32[1,12]{1,0:T(1,128)} %lengths.1) | copy-start | bytes 148
  160.2 75.6 %all-to-all-start = ((bf16[16,24,4096]{2,1,0:T(8,128)(2,1)}), bf16[16,24,4096]{2,1,0:T(8,128)(2,1)S(1)}, u32[]{:S(2)}, u32[]{:S(2)}) async-start(bf16[16,24,4096]{2,1,0:T(8,128)(2,1)} %bitcast.18), calls=%async_computation | async-start | bytes 6291456 | tf_op jit(solution)/shard_map/all_to_all | solution.py:428
  164.7 1.2 copy-start.5
  166.0 1.7 copy-start.14
  167.6 68.2 %copy-start.2 = (s32[128,2]{0,1:T(2,128)S(1)}, s32[128,2]{0,1:T(2,128)}, u32[]{:S(2)}) copy-start(s32[128,2]{0,1:T(2,128)} %param.17) | copy-start | bytes 3076
  167.6 68.2 %copy-start.3 = (f32[128,2]{0,1:T(2,128)S(1)}, f32[128,2]{0,1:T(2,128)}, u32[]{:S(2)}) copy-start(f32[128,2]{0,1:T(2,128)} %param.18) | copy-start | bytes 3076

commit v2 on v1

v2 whole, which is shorter than its diff:
```python
import math

import jax
import jax.numpy as jnp
from jax import lax
from jax.experimental import pallas as pl
from jax.experimental.pallas import tpu as pltpu
from jax.sharding import PartitionSpec as P

MESH = pl.DeviceIdType.MESH
HEAD_WIDTH = 128
QUERY_HEADS = 32
KEY_HEADS = 2
SIDE = 4
DEPTH = 8
QUARTERS = 4
CAP = 24
HEADS_AT_ONCE = 4
TURNED = (((1,), (1,)), ((), ()))


def place():
    dp, ctx, ex = lax.axis_index("dp"), lax.axis_index("ctx"), lax.axis_index("exp")
    return (ctx % 2) * 2 + dp, ctx // 2, ex // 2, ex % 2


def device_at(x, y, ex):
    return (x % 2, y * 2 + x // 2, ex)


def slot_hits(routes):
    experts, tokens = 16, routes.shape[1]
    ids = lax.broadcasted_iota(jnp.int32, (experts, tokens), 0)
    hits = ((ids == routes[0:1, :]) | (ids == routes[1:2, :])).astype(jnp.float32)
    earlier = (
        lax.broadcasted_iota(jnp.int32, (tokens, tokens), 0)
        < lax.broadcasted_iota(jnp.int32, (tokens, tokens), 1)
    ).astype(jnp.bfloat16)
    ranks = jnp.dot(hits.astype(jnp.bfloat16), earlier, preferred_element_type=jnp.float32)
    ranks = jnp.where(hits > 0, ranks, -1.0).astype(jnp.int32)
    wanted = lax.broadcasted_iota(jnp.int32, (experts, CAP, tokens), 1)
    return (ranks[:, None, :] == wanted).astype(jnp.float32)


def attention_bias(lengths, tokens, bias):
    ctx, ex = lax.axis_index("ctx"), lax.axis_index("exp")
    query_pos = (ctx * 16 + ex) * tokens + lax.broadcasted_iota(jnp.int32, (tokens, 1), 0)
    begin = jnp.zeros_like(query_pos)
    bound = jnp.int32(0)
    for r in range(lengths.shape[1]):
        bound = bound + lengths[0, r]
        begin = jnp.where(query_pos >= bound, bound, begin)
    first = (ctx * 16 + (ex // 2) * 2 - 16) * tokens
    step = 256
    for c in range(bias.shape[1] // step):
        key_pos = first + c * step + lax.broadcasted_iota(jnp.int32, (tokens, step), 1)
        seen = (key_pos <= query_pos) & (key_pos >= begin)
        bias[:, c * step:(c + 1) * step] = jnp.where(seen, 0.0, -1e30)


def attend(i, queries, window, bias, out):
    tokens, keys = bias.shape
    columns = HEADS_AT_ONCE * HEAD_WIDTH
    place_of = pl.multiple_of(i * columns, columns)
    group = i // (QUERY_HEADS // KEY_HEADS // HEADS_AT_ONCE)
    key_col = pl.multiple_of(group * HEAD_WIDTH, HEAD_WIDTH)
    value_col = pl.multiple_of((KEY_HEADS + group) * HEAD_WIDTH, HEAD_WIDTH)
    key_rows = window[:, :, :, pl.ds(key_col, HEAD_WIDTH)].reshape(keys, HEAD_WIDTH)
    value_rows = window[:, :, :, pl.ds(value_col, HEAD_WIDTH)].reshape(keys, HEAD_WIDTH)
    block = queries[:, pl.ds(place_of, columns)]
    stacked = jnp.concatenate(
        [block[:, h * HEAD_WIDTH:(h + 1) * HEAD_WIDTH] for h in range(HEADS_AT_ONCE)], axis=0
    )
    scores = lax.dot_general(stacked, key_rows, TURNED, preferred_element_type=jnp.float32)
    scores = scores.reshape(HEADS_AT_ONCE, tokens, keys) + bias[...][None]
    top = jnp.max(scores, axis=-1, keepdims=True)
    probs = jnp.exp2((scores - top) * (math.log2(math.e) / math.sqrt(HEAD_WIDTH)))
    total = jnp.sum(probs, axis=-1, keepdims=True)
    summed = jnp.dot(
        probs.reshape(HEADS_AT_ONCE * tokens, keys).astype(jnp.bfloat16), value_rows,
        preferred_element_type=jnp.float32,
    ).reshape(HEADS_AT_ONCE, tokens, HEAD_WIDTH)
    result = (summed / total).astype(out.dtype)
    out[:, pl.ds(place_of, columns)] = jnp.concatenate([result[h] for h in range(HEADS_AT_ONCE)], axis=1)


def kernel(
    w_gate, w_up, w_down, queries, keys, values, hidden, gain, routes, gates, lengths,
    context, mixture,
    wall, window, hidden_rows, query_rows, packed, arrived, results, returned, sums, active, bias,
    local_sem, out_sem, in_sem, route_out, route_in, kv_out, kv_in, back_out, back_in, back_own,
):
    x, y, z, core = place()
    dp, ctx, ex = lax.axis_index("dp"), lax.axis_index("ctx"), lax.axis_index("exp")
    right, left = lax.rem(x + 1, SIDE), lax.rem(x + SIDE - 1, SIDE)
    above, below = lax.rem(y + 1, SIDE), lax.rem(y + SIDE - 1, SIDE)
    across, over = lax.rem(x + 2, SIDE), lax.rem(y + 2, SIDE)
    to_right, to_left = device_at(right, y, ex), device_at(left, y, ex)
    to_above, to_below = device_at(x, above, ex), device_at(x, below, ex)
    next_ctx, prior_ctx = lax.rem(ctx + 1, 8), lax.rem(ctx + 7, 8)
    sibling = z * 2 + 1 - core
    quarter = wall.shape[-1]
    count = arrived.shape[0] * arrived.shape[1]
    mine = y * SIDE + x

    local = []
    for m, source in enumerate((w_gate, w_up, w_down)):
        for q in range(QUARTERS):
            copy = pltpu.make_async_copy(
                source.at[:, pl.ds(q * quarter, quarter)], wall.at[m, q, mine], local_sem.at[m * QUARTERS + q]
            )
            copy.start()
            local.append(copy)
    width = keys.shape[1]
    key_copy = pltpu.make_async_copy(keys, window.at[DEPTH, core, :, pl.ds(0, width)], local_sem.at[12])
    value_copy = pltpu.make_async_copy(values, window.at[DEPTH, core, :, pl.ds(width, width)], local_sem.at[13])
    hidden_copy = pltpu.make_async_copy(hidden, hidden_rows, local_sem.at[14])
    query_copy = pltpu.make_async_copy(queries, query_rows, local_sem.at[15])
    for copy in (key_copy, value_copy, hidden_copy, query_copy):
        copy.start()

    barrier = pltpu.get_barrier_semaphore()
    for neighbour in (to_right, to_left, to_above, to_below):
        pl.semaphore_signal(barrier, inc=1, device_id=neighbour, device_id_type=MESH)
    for step in range(1, 16):
        pl.semaphore_signal(barrier, inc=1, device_id=(dp, ctx, lax.rem(ex + step, 16)), device_id_type=MESH)
    pl.semaphore_signal(barrier, inc=1, device_id=(dp, prior_ctx, ex), device_id_type=MESH)
    pl.semaphore_wait(barrier, 4 + 15 + 1)

    sent = []
    counts = [0, 0, 0]

    def send(m, first, number, shard, target):
        part = wall.at[m, pl.ds(first, number), shard]
        copy = pltpu.make_async_remote_copy(
            src_ref=part, dst_ref=part,
            send_sem=out_sem.at[m, counts[m]], recv_sem=in_sem.at[m, shard, first],
            device_id=target, device_id_type=MESH,
        )
        counts[m] += 1
        copy.start()
        sent.append(copy)

    def landed(m, first, number, shard):
        part = wall.at[m, pl.ds(first, number), shard]
        pltpu.make_async_copy(part, part, in_sem.at[m, shard, first]).wait()

    def at(shard_x, shard_y):
        return shard_y * SIDE + shard_x

    def first_round(m):
        for copy in local[m * QUARTERS:(m + 1) * QUARTERS]:
            copy.wait()
        for target in (to_right, to_left, to_above, to_below):
            send(m, 0, 4, mine, target)

    def second_round(m):
        landed(m, 0, 4, at(left, y))
        send(m, 0, 2, at(left, y), to_right)
        send(m, 1, 2, at(left, y), to_above)
        send(m, 1, 2, at(left, y), to_below)
        landed(m, 0, 4, at(right, y))
        send(m, 2, 2, at(right, y), to_left)
        send(m, 1, 2, at(right, y), to_above)
        send(m, 1, 2, at(right, y), to_below)
        landed(m, 0, 4, at(x, below))
        send(m, 0, 2, at(x, below), to_above)
        for q in (0, 3):
            send(m, q, 1, at(x, below), to_right)
            send(m, q, 1, at(x, below), to_left)
        landed(m, 0, 4, at(x, above))
        send(m, 2, 2, at(x, above), to_below)
        for q in (0, 3):
            send(m, q, 1, at(x, above), to_right)
            send(m, q, 1, at(x, above), to_left)

    def third_round(m):
        landed(m, 0, 2, at(across, y))
        send(m, 1, 1, at(across, y), to_above)
        send(m, 1, 1, at(across, y), to_below)
        landed(m, 2, 2, at(across, y))
        send(m, 2, 1, at(across, y), to_above)
        send(m, 2, 1, at(across, y), to_below)
        landed(m, 0, 2, at(x, over))
        send(m, 0, 1, at(x, over), to_right)
        send(m, 0, 1, at(x, over), to_left)
        landed(m, 2, 2, at(x, over))
        send(m, 3, 1, at(x, over), to_right)
        send(m, 3, 1, at(x, over), to_left)
        for side in (left, right):
            landed(m, 1, 2, at(side, below))
            send(m, 1, 1, at(side, below), to_above)
            landed(m, 1, 2, at(side, above))
            send(m, 2, 1, at(side, above), to_below)
        for side in (below, above):
            landed(m, 0, 1, at(left, side))
            landed(m, 3, 1, at(left, side))
            send(m, 0, 1, at(left, side), to_right)
            landed(m, 0, 1, at(right, side))
            landed(m, 3, 1, at(right, side))
            send(m, 3, 1, at(right, side), to_left)

    def fourth_round(m):
        landed(m, 1, 1, at(across, below))
        landed(m, 2, 1, at(across, below))
        send(m, 1, 1, at(across, below), to_above)
        landed(m, 1, 1, at(across, above))
        landed(m, 2, 1, at(across, above))
        send(m, 2, 1, at(across, above), to_below)
        landed(m, 0, 1, at(left, over))
        landed(m, 3, 1, at(left, over))
        send(m, 0, 1, at(left, over), to_right)
        landed(m, 0, 1, at(right, over))
        landed(m, 3, 1, at(right, over))
        send(m, 3, 1, at(right, over), to_left)

    def last_round(m):
        for side in (left, right):
            landed(m, 1, 1, at(side, over))
            landed(m, 2, 1, at(side, over))
        for side in (below, above):
            landed(m, 0, 1, at(across, side))
            landed(m, 3, 1, at(across, side))
        for q in range(QUARTERS):
            landed(m, q, 1, at(across, over))

    def matrix(m, q):
        return wall[m, q].reshape(-1, quarter)

    def project(m):
        @pl.loop(0, QUARTERS)
        def _(q):
            cols = pl.ds(pl.multiple_of(q * quarter, quarter), quarter)
            part = lax.dot_general(
                arrived[:, :, cols].reshape(count, quarter), matrix(m, q), TURNED, preferred_element_type=jnp.float32
            )
            sums[m] = jnp.where(q == 0, part, sums[m] + part)

    first_round(0)
    first_round(1)
    key_copy.wait()
    value_copy.wait()
    kv_copies = []
    copy = pltpu.make_async_remote_copy(
        src_ref=window.at[DEPTH, core], dst_ref=window.at[0, core],
        send_sem=kv_out.at[0], recv_sem=kv_in.at[0],
        device_id=(dp, next_ctx, ex), device_id_type=MESH,
    )
    copy.start()
    kv_copies.append(copy)

    hidden_copy.wait()
    picks = slot_hits(routes[...]).reshape(count, -1).astype(jnp.bfloat16)
    rows = hidden_rows[...].astype(jnp.float32)
    scale = lax.rsqrt(jnp.mean(rows * rows, axis=-1, keepdims=True) + 1e-06)
    for q in range(QUARTERS):
        cols = pl.ds(q * quarter, quarter)
        normed = (hidden_rows[:, cols].astype(jnp.float32) * scale * gain[:, cols]).astype(jnp.bfloat16)
        block = jnp.dot(picks, normed, preferred_element_type=jnp.float32).astype(jnp.bfloat16)
        packed[:, :, cols] = block.reshape(16, CAP, quarter)
    own_rows = pltpu.make_async_copy(packed.at[ex], arrived.at[ex], local_sem.at[16])
    own_rows.start()
    route_copies = []
    far_first = (8, 7, 9, 6, 10, 5, 11, 4, 12, 3, 13, 2, 14, 1, 15)
    for step in far_first:
        peer = lax.rem(ex + step, 16)
        copy = pltpu.make_async_remote_copy(
            src_ref=packed.at[peer], dst_ref=arrived.at[ex],
            send_sem=route_out.at[step - 1], recv_sem=route_in.at[ex],
            device_id=(dp, ctx, peer), device_id_type=MESH,
        )
        copy.start()
        route_copies.append(copy)

    second_round(0)
    first_round(2)
    second_round(1)
    third_round(0)
    second_round(2)

    pltpu.make_async_copy(window.at[0, core], window.at[0, core], kv_in.at[0]).wait()
    for step in range(1, DEPTH):
        wraps = (z + step) // DEPTH
        copy = pltpu.make_async_remote_copy(
            src_ref=window.at[DEPTH * (1 - wraps), core], dst_ref=window.at[DEPTH - step, core],
            send_sem=kv_out.at[step], recv_sem=kv_in.at[DEPTH - step],
            device_id=(dp, ctx, lax.rem(z + step, DEPTH) * 2 + core), device_id_type=MESH,
        )
        copy.start()
        kv_copies.append(copy)

    third_round(1)
    fourth_round(0)
    third_round(2)
    fourth_round(1)
    last_round(0)
    own_rows.wait()
    for step in range(1, 16):
        peer = lax.rem(ex + step, 16)
        pltpu.make_async_copy(arrived.at[peer], arrived.at[peer], route_in.at[peer]).wait()
    project(0)
    fourth_round(2)
    last_round(1)
    project(1)
    g = sums[0]
    active[...] = (g / (1.0 + jnp.exp(-g)) * sums[1]).astype(jnp.bfloat16)
    last_round(2)

    back_copies = []
    for q in range(QUARTERS):
        block = jnp.dot(active[...], matrix(2, q), preferred_element_type=jnp.float32)
        results[q] = block.astype(jnp.bfloat16).reshape(16, CAP, quarter)
        own = pltpu.make_async_copy(results.at[q, ex], returned.at[q, ex], back_own.at[q])
        own.start()
        local.append(own)
        for step in far_first:
            peer = lax.rem(ex + step, 16)
            copy = pltpu.make_async_remote_copy(
                src_ref=results.at[q, peer], dst_ref=returned.at[q, ex],
                send_sem=back_out.at[q, step - 1], recv_sem=back_in.at[q, ex],
                device_id=(dp, ctx, peer), device_id_type=MESH,
            )
            copy.start()
            back_copies.append(copy)

    for slot in range(1, DEPTH):
        pltpu.make_async_copy(window.at[slot, core], window.at[slot, core], kv_in.at[slot]).wait()
    share = pltpu.make_async_remote_copy(
        src_ref=window.at[:, core], dst_ref=window.at[:, core],
        send_sem=kv_out.at[DEPTH], recv_sem=kv_in.at[DEPTH],
        device_id=(dp, ctx, sibling), device_id_type=MESH,
    )
    share.start()
    attention_bias(lengths, query_rows.shape[0], bias)
    query_copy.wait()
    pltpu.make_async_copy(window.at[:, 1 - core], window.at[:, 1 - core], kv_in.at[DEPTH]).wait()

    @pl.loop(0, QUERY_HEADS // HEADS_AT_ONCE)
    def _(i):
        attend(i, query_rows, window, bias, context)

    ids = lax.broadcasted_iota(jnp.int32, (16, routes.shape[1]), 0)
    weight = jnp.where(ids == routes[0:1, :], gates[0:1, :], 0.0)
    weight = weight + jnp.where(ids == routes[1:2, :], gates[1:2, :], 0.0)
    spread = (slot_hits(routes[...]) * weight[:, None, :]).reshape(count, -1)
    high = spread.astype(jnp.bfloat16)
    low = (spread - high.astype(jnp.float32)).astype(jnp.bfloat16)
    by_slot = (((0,), (0,)), ((), ()))
    for q in range(QUARTERS):
        local[3 * QUARTERS + q].wait()
        for step in range(1, 16):
            peer = lax.rem(ex + step, 16)
            pltpu.make_async_copy(returned.at[q, peer], returned.at[q, peer], back_in.at[q, peer]).wait()
        block = returned[q].reshape(count, quarter)
        total = lax.dot_general(high, block, by_slot, preferred_element_type=jnp.float32)
        total = total + lax.dot_general(low, block, by_slot, preferred_element_type=jnp.float32)
        mixture[:, q * quarter:(q + 1) * quarter] = total.astype(mixture.dtype)

    share.wait_send()
    for copy in kv_copies + route_copies + sent + back_copies:
        copy.wait_send()


def shards(queries, keys, values, lengths, hidden, norm_gain, routes, gates, w_gate, w_up, w_down):
    tokens, width = hidden.shape
    turned = [jnp.swapaxes(w[0], 0, 1) for w in (w_gate, w_up, w_down)]
    piece, quarter = turned[0].shape[0], width // QUARTERS
    units, count = piece * SIDE * SIDE, 16 * CAP
    far, vmem = pl.BlockSpec(memory_space=pltpu.HBM), pl.BlockSpec(memory_space=pltpu.VMEM)
    bf16, f32, dma = jnp.bfloat16, jnp.float32, pltpu.SemaphoreType.DMA
    out = jax.ShapeDtypeStruct((tokens, width), bf16)
    return pl.pallas_call(
        kernel,
        out_shape=(out, out),
        in_specs=[far] * 7 + [vmem] * 3 + [pl.BlockSpec(memory_space=pltpu.SMEM)],
        out_specs=[vmem] * 2,
        scratch_shapes=[
            pltpu.VMEM((3, QUARTERS, SIDE * SIDE, piece, quarter), bf16),
            pltpu.VMEM((DEPTH + 1, 2, tokens, 2 * keys.shape[1]), bf16),
            pltpu.VMEM((tokens, width), bf16),
            pltpu.VMEM((tokens, width), bf16),
            pltpu.VMEM((16, CAP, width), bf16),
            pltpu.VMEM((16, CAP, width), bf16),
            pltpu.VMEM((QUARTERS, 16, CAP, quarter), bf16),
            pltpu.VMEM((QUARTERS, 16, CAP, quarter), bf16),
            pltpu.VMEM((2, count, units), f32),
            pltpu.VMEM((count, units), bf16),
            pltpu.VMEM((tokens, (DEPTH + 1) * 2 * tokens), f32),
            dma((17,)), dma((3, 40)), dma((3, 16, 4)), dma((15,)), dma((16,)), dma((9,)), dma((9,)),
            dma((QUARTERS, 15)), dma((QUARTERS, 16)), dma((QUARTERS,)),
        ],
        compiler_params=pltpu.CompilerParams(
            collective_id=0, has_side_effects=True, vmem_limit_bytes=60 * 1024 * 1024
        ),
        cost_estimate=pl.CostEstimate(flops=20 * 10**9, bytes_accessed=10 * 10**6, transcendentals=10**7),
        name="whole_block",
    )(*turned, queries, keys, values, hidden, norm_gain[None, :], routes.T, gates.T, lengths)


def solution(mesh):
    whole = P(("dp", "ctx", "exp"), None)
    weights = P("exp", None, ("dp", "ctx"))
    return jax.shard_map(
        shards,
        mesh=mesh,
        in_specs=(whole, whole, whole, P("dp", None), whole, P(), whole, whole, weights, weights, weights),
        out_specs=(whole, whole),
        check_vma=False,
    )
```

time: 240 us -> 193 us (0.80)
  waiting for transfers between devices: 39 us -> 0 us
  local copies, waits for them, and re-layouts: 13.2 us -> 3.35 us
  Pallas kernels: 182 us -> 189 us
  starting transfers between devices: 4.55 us -> 0 us
    all_to_all x1 -> x0, waiting for transfers between devices: 39 us -> none  [shards(): lax.all_to_all(results.reshape(16, CAP, width), 'exp', split_axis=0, conc...]
    unnamed x30 -> x4, local copies, waits for them, and re-layouts: 13.2 us -> 3.35 us
    pallas_call x4 -> x1, Pallas kernels: 182 us -> 189 us  [shards(): pl.pallas_call(kernel, out_shape=(out, out), in_specs=[far] * 7 + [vmem]...]
    all_to_all x1 -> x0, starting transfers between devices: 4.55 us -> none  [shards(): lax.all_to_all(results.reshape(16, CAP, width), 'exp', split_axis=0, conc...]
  transfers between devices with their start and end apart: 1 -> 0, of which waited for: 1 -> 0; matrix products, arithmetic and copies ran while one was open for 0% -> 0% of each run, Pallas kernels for 12% -> 0%
where the time goes in v2:
time: 193 us
  Pallas kernels  189 us (98%)
  local copies, waits for them, and re-layouts  3.35 us (2%)
    pallas_call x1, Pallas kernels, shards(): pl.pallas_call(kernel, out_shape=(out, out), in_specs=[far] * 7 + [vmem]...  189 us

profile of v2, /device:TPU:1, one launch (start us, length us, event | category | flops | bytes accessed | tf_op | source)
XLA Modules:
  0.0 192.7 jit_solution(17540026431437875999)
XLA Ops:
  0.6 188.7 %whole_block.1 = (bf16[128,4096]{1,0:T(8,128)(2,1)}, bf16[128,4096]{1,0:T(8,128)(2,1)}) custom-call(bf16[48,4096]{1,0:T(8,128)(2,1)} %bitcast.12, bf16[48,4096]{1,0:T(8,128)(2,1)} %bitcast.13, bf16[48,4096]{1,0:T(8,128)(2,1)} %bitcast.14, bf16[128,4096]{1,0:T(8,128)(2,1)} %queries.1, bf16[128,256]{1,0:T(8,128)(2,1)} %keys.1, bf16[128,256]{1,0:T(8,128)(2,1)} %values.1, ...), custom_call_target="tpu_custom_call" | custom-call | flops 20000000000 | bytes 10000000 | tf_op jit(solution)/shard_map/whole_block/pallas_call | solution.py:372
  189.4 0.0 copy-start
  189.4 2.4 %copy.15 = bf16[128,4096]{1,0:T(8,128)(2,1)} copy(bf16[128,4096]{1,0:T(8,128)(2,1)} %get-tuple-element.4) | data formatting | bytes 2097152
  191.8 0.0 copy-done
  191.8 1.0 copy.16
Async XLA Ops:
  189.4 2.4 %copy-start = (bf16[128,4096]{1,0:T(8,128)(2,1)S(1)}, bf16[128,4096]{1,0:T(8,128)(2,1)}, u32[]{:S(2)}) copy-start(bf16[128,4096]{1,0:T(8,128)(2,1)} %get-tuple-element.5) | copy-start | bytes 3145732

commit v3 on v2

v3 whole, which is shorter than its diff:
```python
import math

import jax
import jax.numpy as jnp
from jax import lax
from jax.experimental import pallas as pl
from jax.experimental.pallas import tpu as pltpu
from jax.sharding import PartitionSpec as P

MESH = pl.DeviceIdType.MESH
HEAD_WIDTH = 128
QUERY_HEADS = 32
KEY_HEADS = 2
SIDE = 4
DEPTH = 8
QUARTERS = 4
CAP = 24
HEADS_AT_ONCE = 4
TURNED = (((1,), (1,)), ((), ()))


def place():
    dp, ctx, ex = lax.axis_index("dp"), lax.axis_index("ctx"), lax.axis_index("exp")
    return (ctx % 2) * 2 + dp, ctx // 2, ex // 2, ex % 2


def device_at(x, y, ex):
    return (x % 2, y * 2 + x // 2, ex)


def slot_hits(routes):
    experts, tokens = 16, routes.shape[1]
    ids = lax.broadcasted_iota(jnp.int32, (experts, tokens), 0)
    hits = ((ids == routes[0:1, :]) | (ids == routes[1:2, :])).astype(jnp.float32)
    earlier = (
        lax.broadcasted_iota(jnp.int32, (tokens, tokens), 0)
        < lax.broadcasted_iota(jnp.int32, (tokens, tokens), 1)
    ).astype(jnp.bfloat16)
    ranks = jnp.dot(hits.astype(jnp.bfloat16), earlier, preferred_element_type=jnp.float32)
    ranks = jnp.where(hits > 0, ranks, -1.0).astype(jnp.int32)
    wanted = lax.broadcasted_iota(jnp.int32, (experts, CAP, tokens), 1)
    return (ranks[:, None, :] == wanted).astype(jnp.float32)


def attention_bias(lengths, tokens, bias):
    ctx, ex = lax.axis_index("ctx"), lax.axis_index("exp")
    query_pos = (ctx * 16 + ex) * tokens + lax.broadcasted_iota(jnp.int32, (tokens, 1), 0)
    begin = jnp.zeros_like(query_pos)
    bound = jnp.int32(0)
    for r in range(lengths.shape[1]):
        bound = bound + lengths[0, r]
        begin = jnp.where(query_pos >= bound, bound, begin)
    first = (ctx * 16 + (ex // 2) * 2 - 16) * tokens
    step = 256
    for c in range(bias.shape[1] // step):
        key_pos = first + c * step + lax.broadcasted_iota(jnp.int32, (tokens, step), 1)
        seen = (key_pos <= query_pos) & (key_pos >= begin)
        bias[:, c * step:(c + 1) * step] = jnp.where(seen, 0.0, -1e30)


def attend(i, queries, window, bias, out):
    tokens, keys = bias.shape
    columns = HEADS_AT_ONCE * HEAD_WIDTH
    place_of = pl.multiple_of(i * columns, columns)
    group = i // (QUERY_HEADS // KEY_HEADS // HEADS_AT_ONCE)
    key_col = pl.multiple_of(group * HEAD_WIDTH, HEAD_WIDTH)
    value_col = pl.multiple_of((KEY_HEADS + group) * HEAD_WIDTH, HEAD_WIDTH)
    key_rows = window[:, :, :, pl.ds(key_col, HEAD_WIDTH)].reshape(keys, HEAD_WIDTH)
    value_rows = window[:, :, :, pl.ds(value_col, HEAD_WIDTH)].reshape(keys, HEAD_WIDTH)
    block = queries[:, pl.ds(place_of, columns)]
    stacked = jnp.concatenate(
        [block[:, h * HEAD_WIDTH:(h + 1) * HEAD_WIDTH] for h in range(HEADS_AT_ONCE)], axis=0
    )
    scores = lax.dot_general(stacked, key_rows, TURNED, preferred_element_type=jnp.float32)
    scores = scores.reshape(HEADS_AT_ONCE, tokens, keys) + bias[...][None]
    top = jnp.max(scores, axis=-1, keepdims=True)
    probs = jnp.exp2((scores - top) * (math.log2(math.e) / math.sqrt(HEAD_WIDTH)))
    total = jnp.sum(probs, axis=-1, keepdims=True)
    summed = jnp.dot(
        probs.reshape(HEADS_AT_ONCE * tokens, keys).astype(jnp.bfloat16), value_rows,
        preferred_element_type=jnp.float32,
    ).reshape(HEADS_AT_ONCE, tokens, HEAD_WIDTH)
    result = (summed / total).astype(out.dtype)
    out[:, pl.ds(place_of, columns)] = jnp.concatenate([result[h] for h in range(HEADS_AT_ONCE)], axis=1)


def kernel(
    w_gate, w_up, w_down, queries, keys, values, hidden, gain, routes, gates, lengths,
    context, mixture,
    wall, window, hidden_rows, query_rows, packed, arrived, results, returned, sums, active, bias,
    local_sem, pass_sem, first_sem, out_sem, in_sem, route_out, route_in, kv_out, kv_in, back_out, back_in,
):
    x, y, z, core = place()
    dp, ctx, ex = lax.axis_index("dp"), lax.axis_index("ctx"), lax.axis_index("exp")
    group, partner = x // 2, SIDE - 1 - x
    native = core == group
    beside = x + 1 - 2 * (x % 2)
    above, below, over = lax.rem(y + 1, SIDE), lax.rem(y + SIDE - 1, SIDE), lax.rem(y + 2, SIDE)
    to_beside, to_above, to_below = device_at(beside, y, ex), device_at(x, above, ex), device_at(x, below, ex)
    sibling = z * 2 + 1 - core
    to_sibling = (dp, ctx, sibling)
    prior_ctx, next_ctx = lax.rem(ctx + 7, 8), lax.rem(ctx + 1, 8)
    expert = z * 2 + group
    rows_x = jnp.where(native, x, partner)
    quarter = wall.shape[-1]
    count = arrived.shape[1] * arrived.shape[2]

    def at(chip_x, chip_y):
        return chip_y * SIDE + jnp.where(native, chip_x, SIDE - 1 - chip_x)

    def shard_copies(remote):
        copies = []
        for m, source in enumerate((w_gate, w_up, w_down)):
            for q in range(QUARTERS):
                part = source.at[:, pl.ds(q * quarter, quarter)]
                home, arrival = wall.at[m, q, y * SIDE + x], in_sem.at[m, y * SIDE + x, q]
                if remote:
                    copies.append(pltpu.make_async_remote_copy(
                        src_ref=part, dst_ref=home, send_sem=pass_sem.at[m, q], recv_sem=arrival,
                        device_id=device_at(partner, y, sibling), device_id_type=MESH,
                    ))
                else:
                    copies.append(pltpu.make_async_copy(part, home, arrival))
        return copies

    @pl.when(native)
    def _():
        for copy in shard_copies(False):
            copy.start()

    width = keys.shape[1]
    key_copy = pltpu.make_async_copy(keys, window.at[DEPTH, core, :, pl.ds(0, width)], local_sem.at[0])
    value_copy = pltpu.make_async_copy(values, window.at[DEPTH, core, :, pl.ds(width, width)], local_sem.at[1])
    hidden_copy = pltpu.make_async_copy(hidden, hidden_rows, local_sem.at[2])
    query_copy = pltpu.make_async_copy(queries, query_rows, local_sem.at[3])
    for copy in (hidden_copy, key_copy, value_copy, query_copy):
        copy.start()

    barrier = pltpu.get_barrier_semaphore()
    for neighbour in (to_beside, to_above, to_below, (dp, prior_ctx, ex)):
        pl.semaphore_signal(barrier, inc=1, device_id=neighbour, device_id_type=MESH)
    for step in range(16):
        other = lax.rem(ex + step, 16)
        if step:
            pl.semaphore_signal(barrier, inc=1, device_id=(dp, ctx, other), device_id_type=MESH)
        pl.semaphore_signal(barrier, inc=1, device_id=device_at(partner, y, other), device_id_type=MESH)
    pl.semaphore_wait(barrier, 4 + 15 + 16)

    @pl.when(jnp.logical_not(native))
    def _():
        for copy in shard_copies(True):
            copy.start()

    sent = []
    counts = [0, 0, 0]

    def send(m, first, number, shard, target):
        part = wall.at[m, pl.ds(first, number), shard]
        copy = pltpu.make_async_remote_copy(
            src_ref=part, dst_ref=part,
            send_sem=out_sem.at[m, counts[m]], recv_sem=in_sem.at[m, shard, first],
            device_id=target, device_id_type=MESH,
        )
        counts[m] += 1
        copy.start()
        sent.append(copy)

    def landed(m, first, number, shard):
        part = wall.at[m, pl.ds(first, number), shard]
        pltpu.make_async_copy(part, part, in_sem.at[m, shard, first]).wait()

    def first_copies(m):
        part = wall.at[m, :, at(x, y)]
        return [
            pltpu.make_async_remote_copy(
                src_ref=part, dst_ref=part, send_sem=first_sem.at[m, i], recv_sem=in_sem.at[m, at(x, y), 0],
                device_id=target, device_id_type=MESH,
            )
            for i, target in enumerate((to_beside, to_above, to_below, to_sibling))
        ]

    def share_shard(m, shard):
        send(m, 0, 4, shard, to_sibling)

    def first_round(m):
        for q in range(QUARTERS):
            landed(m, q, 1, at(x, y))
        for copy in first_copies(m):
            copy.start()

    def second_round(m):
        landed(m, 0, 4, at(beside, y))
        send(m, 1, 2, at(beside, y), to_above)
        send(m, 1, 2, at(beside, y), to_below)
        landed(m, 0, 4, at(x, below))
        send(m, 0, 2, at(x, below), to_above)
        send(m, 0, 1, at(x, below), to_beside)
        send(m, 3, 1, at(x, below), to_beside)
        landed(m, 0, 4, at(x, above))
        send(m, 2, 2, at(x, above), to_below)
        send(m, 0, 1, at(x, above), to_beside)
        send(m, 3, 1, at(x, above), to_beside)
        for shard in (at(beside, y), at(x, below), at(x, above)):
            share_shard(m, shard)

    def third_round(m):
        landed(m, 0, 2, at(x, over))
        send(m, 0, 1, at(x, over), to_beside)
        landed(m, 2, 2, at(x, over))
        send(m, 3, 1, at(x, over), to_beside)
        landed(m, 1, 2, at(beside, below))
        send(m, 1, 1, at(beside, below), to_above)
        landed(m, 1, 2, at(beside, above))
        send(m, 2, 1, at(beside, above), to_below)
        share_shard(m, at(x, over))
        for side in (below, above):
            landed(m, 0, 1, at(beside, side))
            landed(m, 3, 1, at(beside, side))
            share_shard(m, at(beside, side))

    def fourth_round(m):
        for q in range(QUARTERS):
            landed(m, q, 1, at(beside, over))
        share_shard(m, at(beside, over))

    def last_round(m):
        for row in range(SIDE):
            for chip in (x, beside):
                landed(m, 0, 4, row * SIDE + jnp.where(native, SIDE - 1 - chip, chip))

    def matrix(m, q):
        return wall[m, q].reshape(-1, quarter)

    def project(m):
        @pl.loop(0, QUARTERS)
        def _(q):
            part = lax.dot_general(
                arrived[q].reshape(count, quarter), matrix(m, q), TURNED, preferred_element_type=jnp.float32
            )
            sums[m] = jnp.where(q == 0, part, sums[m] + part)

    def route_copy(q, step, c):
        plane = lax.rem(z + step, DEPTH)
        wanted = plane * 2 + (group if c == 0 else 1 - group)
        return pltpu.make_async_remote_copy(
            src_ref=packed.at[q, wanted], dst_ref=arrived.at[q, ex],
            send_sem=route_out.at[q, 2 * step + c], recv_sem=route_in.at[q, ex],
            device_id=device_at(x if c == 0 else partner, y, plane * 2 + group), device_id_type=MESH,
        )

    def back_copy(q, step, c):
        source = lax.rem(z + step, DEPTH) * 2 + (core if c == 0 else 1 - core)
        return pltpu.make_async_remote_copy(
            src_ref=results.at[q, source], dst_ref=returned.at[q, expert],
            send_sem=back_out.at[q, 2 * step + c], recv_sem=back_in.at[q, expert],
            device_id=device_at(rows_x, y, source), device_id_type=MESH,
        )

    far_first = (4, 3, 5, 2, 6, 1, 7, 0)

    def scatter(make, q, own):
        for step in far_first:
            for c in (0, 1):
                if step or c:
                    make(q, step, c).start()

        @pl.when(native)
        def _():
            own.start()

        @pl.when(jnp.logical_not(native))
        def _():
            make(q, 0, 0).start()

    def scattered(make, q):
        for step in far_first:
            for c in (0, 1):
                if step or c:
                    make(q, step, c).wait_send()

        @pl.when(jnp.logical_not(native))
        def _():
            make(q, 0, 0).wait_send()

    @pl.when(native)
    def _():
        first_round(0)
        first_round(1)

    key_copy.wait()
    value_copy.wait()
    kv_copies = []
    copy = pltpu.make_async_remote_copy(
        src_ref=window.at[DEPTH, core], dst_ref=window.at[0, core],
        send_sem=kv_out.at[0], recv_sem=kv_in.at[0],
        device_id=(dp, next_ctx, ex), device_id_type=MESH,
    )
    copy.start()
    kv_copies.append(copy)

    hidden_copy.wait()
    picks = slot_hits(routes[...]).reshape(count, -1).astype(jnp.bfloat16)
    rows = hidden_rows[...].astype(jnp.float32)
    scale = lax.rsqrt(jnp.mean(rows * rows, axis=-1, keepdims=True) + 1e-06)
    for q in range(QUARTERS):
        cols = pl.ds(q * quarter, quarter)
        normed = (hidden_rows[:, cols].astype(jnp.float32) * scale * gain[:, cols]).astype(jnp.bfloat16)
        block = jnp.dot(picks, normed, preferred_element_type=jnp.float32).astype(jnp.bfloat16)
        packed[q] = block.reshape(16, CAP, quarter)
        scatter(route_copy, q, pltpu.make_async_copy(packed.at[q, ex], arrived.at[q, ex], route_in.at[q, ex]))

    @pl.when(jnp.logical_not(native))
    def _():
        first_round(0)
        first_round(1)

    second_round(0)
    first_round(2)
    second_round(1)
    third_round(0)
    second_round(2)
    third_round(1)
    fourth_round(0)
    third_round(2)
    fourth_round(1)
    last_round(0)
    fourth_round(2)
    for q in range(QUARTERS):
        scattered(route_copy, q)

    pltpu.make_async_copy(window.at[0, core], window.at[0, core], kv_in.at[0]).wait()
    for step in range(1, DEPTH):
        wraps = (z + step) // DEPTH
        copy = pltpu.make_async_remote_copy(
            src_ref=window.at[DEPTH * (1 - wraps), core], dst_ref=window.at[DEPTH - step, core],
            send_sem=kv_out.at[step], recv_sem=kv_in.at[DEPTH - step],
            device_id=(dp, ctx, lax.rem(z + step, DEPTH) * 2 + core), device_id_type=MESH,
        )
        copy.start()
        kv_copies.append(copy)

    for q in range(QUARTERS):
        for source in range(16):
            pltpu.make_async_copy(arrived.at[q, source], arrived.at[q, source], route_in.at[q, source]).wait()
    project(0)
    last_round(1)
    project(1)
    g = sums[0]
    active[...] = (g / (1.0 + jnp.exp(-g)) * sums[1]).astype(jnp.bfloat16)
    last_round(2)

    for q in range(QUARTERS):
        block = jnp.dot(active[...], matrix(2, q), preferred_element_type=jnp.float32)
        results[q] = block.astype(jnp.bfloat16).reshape(16, CAP, quarter)
        scatter(back_copy, q, pltpu.make_async_copy(results.at[q, ex], returned.at[q, ex], back_in.at[q, ex]))

    for slot in range(1, DEPTH):
        pltpu.make_async_copy(window.at[slot, core], window.at[slot, core], kv_in.at[slot]).wait()
    share = pltpu.make_async_remote_copy(
        src_ref=window.at[:, core], dst_ref=window.at[:, core],
        send_sem=kv_out.at[DEPTH], recv_sem=kv_in.at[DEPTH],
        device_id=to_sibling, device_id_type=MESH,
    )
    share.start()
    attention_bias(lengths, query_rows.shape[0], bias)
    query_copy.wait()
    pltpu.make_async_copy(window.at[:, 1 - core], window.at[:, 1 - core], kv_in.at[DEPTH]).wait()

    @pl.loop(0, QUERY_HEADS // HEADS_AT_ONCE)
    def _(i):
        attend(i, query_rows, window, bias, context)

    ids = lax.broadcasted_iota(jnp.int32, (16, routes.shape[1]), 0)
    weight = jnp.where(ids == routes[0:1, :], gates[0:1, :], 0.0)
    weight = weight + jnp.where(ids == routes[1:2, :], gates[1:2, :], 0.0)
    spread = (slot_hits(routes[...]) * weight[:, None, :]).reshape(count, -1)
    high = spread.astype(jnp.bfloat16)
    low = (spread - high.astype(jnp.float32)).astype(jnp.bfloat16)
    by_slot = (((0,), (0,)), ((), ()))
    for q in range(QUARTERS):
        for e in range(16):
            pltpu.make_async_copy(returned.at[q, e], returned.at[q, e], back_in.at[q, e]).wait()
        block = returned[q].reshape(count, quarter)
        total = lax.dot_general(high, block, by_slot, preferred_element_type=jnp.float32)
        total = total + lax.dot_general(low, block, by_slot, preferred_element_type=jnp.float32)
        mixture[:, q * quarter:(q + 1) * quarter] = total.astype(mixture.dtype)

    share.wait_send()
    for m in range(3):
        for copy in first_copies(m):
            copy.wait_send()
    for copy in kv_copies + sent:
        copy.wait_send()
    for q in range(QUARTERS):
        scattered(back_copy, q)

    @pl.when(jnp.logical_not(native))
    def _():
        for copy in shard_copies(True):
            copy.wait_send()


def shards(queries, keys, values, lengths, hidden, norm_gain, routes, gates, w_gate, w_up, w_down):
    tokens, width = hidden.shape
    turned = [jnp.swapaxes(w[0], 0, 1) for w in (w_gate, w_up, w_down)]
    piece, quarter = turned[0].shape[0], width // QUARTERS
    units, count = piece * SIDE * SIDE, 16 * CAP
    far, vmem = pl.BlockSpec(memory_space=pltpu.HBM), pl.BlockSpec(memory_space=pltpu.VMEM)
    bf16, f32, dma = jnp.bfloat16, jnp.float32, pltpu.SemaphoreType.DMA
    out = jax.ShapeDtypeStruct((tokens, width), bf16)
    return pl.pallas_call(
        kernel,
        out_shape=(out, out),
        in_specs=[far] * 7 + [vmem] * 3 + [pl.BlockSpec(memory_space=pltpu.SMEM)],
        out_specs=[vmem] * 2,
        scratch_shapes=[
            pltpu.VMEM((3, QUARTERS, SIDE * SIDE, piece, quarter), bf16),
            pltpu.VMEM((DEPTH + 1, 2, tokens, 2 * keys.shape[1]), bf16),
            pltpu.VMEM((tokens, width), bf16),
            pltpu.VMEM((tokens, width), bf16),
            pltpu.VMEM((QUARTERS, 16, CAP, quarter), bf16),
            pltpu.VMEM((QUARTERS, 16, CAP, quarter), bf16),
            pltpu.VMEM((QUARTERS, 16, CAP, quarter), bf16),
            pltpu.VMEM((QUARTERS, 16, CAP, quarter), bf16),
            pltpu.VMEM((2, count, units), f32),
            pltpu.VMEM((count, units), bf16),
            pltpu.VMEM((tokens, (DEPTH + 1) * 2 * tokens), f32),
            dma((4,)), dma((3, QUARTERS)), dma((3, 4)), dma((3, 20)), dma((3, 16, QUARTERS)), dma((QUARTERS, 16)), dma((QUARTERS, 16)),
            dma((9,)), dma((9,)), dma((QUARTERS, 16)), dma((QUARTERS, 16)),
        ],
        compiler_params=pltpu.CompilerParams(
            collective_id=0, has_side_effects=True, vmem_limit_bytes=60 * 1024 * 1024
        ),
        cost_estimate=pl.CostEstimate(flops=20 * 10**9, bytes_accessed=10 * 10**6, transcendentals=10**7),
        name="whole_block",
    )(*turned, queries, keys, values, hidden, norm_gain[None, :], routes.T, gates.T, lengths)


def solution(mesh):
    whole = P(("dp", "ctx", "exp"), None)
    weights = P("exp", None, ("dp", "ctx"))
    return jax.shard_map(
        shards,
        mesh=mesh,
        in_specs=(whole, whole, whole, P("dp", None), whole, P(), whole, whole, weights, weights, weights),
        out_specs=(whole, whole),
        check_vma=False,
    )
```

time: 193 us -> 184 us (0.953)
  Pallas kernels: 189 us -> 179 us
    pallas_call x1, Pallas kernels: 189 us -> 179 us  [shards(): pl.pallas_call(kernel, out_shape=(out, out), in_specs=[far] * 7 + [vmem]...]
where the time goes in v3:
time: 184 us; the launch traced here: 183 us
  Pallas kernels  179 us (97%)
  local copies, waits for them, and re-layouts  3.35 us (2%)
    pallas_call x1, Pallas kernels, shards(): pl.pallas_call(kernel, out_shape=(out, out), in_specs=[far] * 7 + [vmem]...  179 us

profile of v3, /device:TPU:1, one launch (start us, length us, event | category | flops | bytes accessed | tf_op | source)
XLA Modules:
  0.0 183.4 jit_solution(12157462042941864316)
XLA Ops:
  0.6 179.4 %whole_block.1 = (bf16[128,4096]{1,0:T(8,128)(2,1)}, bf16[128,4096]{1,0:T(8,128)(2,1)}) custom-call(bf16[48,4096]{1,0:T(8,128)(2,1)} %bitcast.12, bf16[48,4096]{1,0:T(8,128)(2,1)} %bitcast.13, bf16[48,4096]{1,0:T(8,128)(2,1)} %bitcast.14, bf16[128,4096]{1,0:T(8,128)(2,1)} %queries.1, bf16[128,256]{1,0:T(8,128)(2,1)} %keys.1, bf16[128,256]{1,0:T(8,128)(2,1)} %values.1, ...), custom_call_target="tpu_custom_call" | custom-call | flops 20000000000 | bytes 10000000 | tf_op jit(solution)/shard_map/whole_block/pallas_call | solution.py:411
  180.0 0.0 copy-start
  180.0 2.4 %copy.15 = bf16[128,4096]{1,0:T(8,128)(2,1)} copy(bf16[128,4096]{1,0:T(8,128)(2,1)} %get-tuple-element.4) | data formatting | bytes 2097152
  182.4 0.0 copy-done
  182.4 1.0 copy.16
Async XLA Ops:
  180.0 2.4 %copy-start = (bf16[128,4096]{1,0:T(8,128)(2,1)S(1)}, bf16[128,4096]{1,0:T(8,128)(2,1)}, u32[]{:S(2)}) copy-start(bf16[128,4096]{1,0:T(8,128)(2,1)} %get-tuple-element.5) | copy-start | bytes 3145732

commit v4 on v3

--- a/solution.py
+++ b/solution.py
@@ -87,8 +87,8 @@
 def kernel(
     w_gate, w_up, w_down, queries, keys, values, hidden, gain, routes, gates, lengths,
     context, mixture,
-    wall, window, hidden_rows, query_rows, packed, arrived, results, returned, sums, active, bias,
-    local_sem, pass_sem, first_sem, out_sem, in_sem, route_out, route_in, kv_out, kv_in, back_out, back_in,
+    wall, window, hidden_rows, query_rows, context_rows, mixture_rows, packed, arrived, results, returned, sums, active, bias,
+    local_sem, pass_out, own_in, out_sem, in_sem, share_in, route_out, route_in, kv_out, kv_in, back_out, back_in,
 ):
     x, y, z, core = place()
     dp, ctx, ex = lax.axis_index("dp"), lax.axis_index("ctx"), lax.axis_index("exp")
@@ -113,10 +113,10 @@
         for m, source in enumerate((w_gate, w_up, w_down)):
             for q in range(QUARTERS):
                 part = source.at[:, pl.ds(q * quarter, quarter)]
-                home, arrival = wall.at[m, q, y * SIDE + x], in_sem.at[m, y * SIDE + x, q]
+                home, arrival = wall.at[m, q, y * SIDE + x], own_in.at[m]
                 if remote:
                     copies.append(pltpu.make_async_remote_copy(
-                        src_ref=part, dst_ref=home, send_sem=pass_sem.at[m, q], recv_sem=arrival,
+                        src_ref=part, dst_ref=home, send_sem=pass_out, recv_sem=arrival,
                         device_id=device_at(partner, y, sibling), device_id_type=MESH,
                     ))
                 else:
@@ -144,6 +144,18 @@
         if step:
             pl.semaphore_signal(barrier, inc=1, device_id=(dp, ctx, other), device_id_type=MESH)
         pl.semaphore_signal(barrier, inc=1, device_id=device_at(partner, y, other), device_id_type=MESH)
+
+    hidden_copy.wait()
+    picks = slot_hits(routes[...]).reshape(count, -1).astype(jnp.bfloat16)
+    rows = hidden_rows[...].astype(jnp.float32)
+    scale = lax.rsqrt(jnp.mean(rows * rows, axis=-1, keepdims=True) + 1e-06)
+    for q in range(QUARTERS):
+        cols = pl.ds(q * quarter, quarter)
+        normed = (hidden_rows[:, cols].astype(jnp.float32) * scale * gain[:, cols]).astype(jnp.bfloat16)
+        block = jnp.dot(picks, normed, preferred_element_type=jnp.float32).astype(jnp.bfloat16)
+        packed[q] = block.reshape(16, CAP, quarter)
+    key_copy.wait()
+    value_copy.wait()
     pl.semaphore_wait(barrier, 4 + 15 + 16)
 
     @pl.when(jnp.logical_not(native))
@@ -151,82 +163,66 @@
         for copy in shard_copies(True):
             copy.start()
 
-    sent = []
-    counts = [0, 0, 0]
-
-    def send(m, first, number, shard, target):
+    def send(m, first, number, shard, target, arrival):
         part = wall.at[m, pl.ds(first, number), shard]
-        copy = pltpu.make_async_remote_copy(
-            src_ref=part, dst_ref=part,
-            send_sem=out_sem.at[m, counts[m]], recv_sem=in_sem.at[m, shard, first],
+        pltpu.make_async_remote_copy(
+            src_ref=part, dst_ref=part, send_sem=out_sem.at[m], recv_sem=arrival,
             device_id=target, device_id_type=MESH,
-        )
-        counts[m] += 1
-        copy.start()
-        sent.append(copy)
-
-    def landed(m, first, number, shard):
+        ).start()
+
+    def landed(m, first, number, shard, index):
         part = wall.at[m, pl.ds(first, number), shard]
-        pltpu.make_async_copy(part, part, in_sem.at[m, shard, first]).wait()
-
-    def first_copies(m):
-        part = wall.at[m, :, at(x, y)]
-        return [
-            pltpu.make_async_remote_copy(
-                src_ref=part, dst_ref=part, send_sem=first_sem.at[m, i], recv_sem=in_sem.at[m, at(x, y), 0],
-                device_id=target, device_id_type=MESH,
-            )
-            for i, target in enumerate((to_beside, to_above, to_below, to_sibling))
-        ]
+        pltpu.make_async_copy(part, part, in_sem.at[m, index]).wait()
+
+    def wait_for(part, semaphore):
+        pltpu.make_async_copy(part, part, semaphore).wait()
 
     def share_shard(m, shard):
-        send(m, 0, 4, shard, to_sibling)
+        send(m, 0, 4, shard, to_sibling, share_in.at[m])
 
     def first_round(m):
-        for q in range(QUARTERS):
-            landed(m, q, 1, at(x, y))
-        for copy in first_copies(m):
-            copy.start()
+        wait_for(wall.at[m, :, at(x, y)], own_in.at[m])
+        for i, target in enumerate((to_beside, to_above, to_below)):
+            send(m, 0, 4, at(x, y), target, in_sem.at[m, i])
+        share_shard(m, at(x, y))
 
     def second_round(m):
-        landed(m, 0, 4, at(beside, y))
-        send(m, 1, 2, at(beside, y), to_above)
-        send(m, 1, 2, at(beside, y), to_below)
-        landed(m, 0, 4, at(x, below))
-        send(m, 0, 2, at(x, below), to_above)
-        send(m, 0, 1, at(x, below), to_beside)
-        send(m, 3, 1, at(x, below), to_beside)
-        landed(m, 0, 4, at(x, above))
-        send(m, 2, 2, at(x, above), to_below)
-        send(m, 0, 1, at(x, above), to_beside)
-        send(m, 3, 1, at(x, above), to_beside)
+        landed(m, 0, 4, at(beside, y), 0)
+        send(m, 1, 2, at(beside, y), to_above, in_sem.at[m, 5])
+        send(m, 1, 2, at(beside, y), to_below, in_sem.at[m, 8])
+        landed(m, 0, 4, at(x, below), 1)
+        send(m, 0, 2, at(x, below), to_above, in_sem.at[m, 3])
+        send(m, 0, 1, at(x, below), to_beside, in_sem.at[m, 6])
+        send(m, 3, 1, at(x, below), to_beside, in_sem.at[m, 7])
+        landed(m, 0, 4, at(x, above), 2)
+        send(m, 2, 2, at(x, above), to_below, in_sem.at[m, 4])
+        send(m, 0, 1, at(x, above), to_beside, in_sem.at[m, 9])
+        send(m, 3, 1, at(x, above), to_beside, in_sem.at[m, 10])
         for shard in (at(beside, y), at(x, below), at(x, above)):
             share_shard(m, shard)
 
     def third_round(m):
-        landed(m, 0, 2, at(x, over))
-        send(m, 0, 1, at(x, over), to_beside)
-        landed(m, 2, 2, at(x, over))
-        send(m, 3, 1, at(x, over), to_beside)
-        landed(m, 1, 2, at(beside, below))
-        send(m, 1, 1, at(beside, below), to_above)
-        landed(m, 1, 2, at(beside, above))
-        send(m, 2, 1, at(beside, above), to_below)
+        landed(m, 0, 2, at(x, over), 3)
+        send(m, 0, 1, at(x, over), to_beside, in_sem.at[m, 11])
+        landed(m, 2, 2, at(x, over), 4)
+        send(m, 3, 1, at(x, over), to_beside, in_sem.at[m, 14])
+        landed(m, 1, 2, at(beside, below), 5)
+        send(m, 1, 1, at(beside, below), to_above, in_sem.at[m, 12])
+        landed(m, 1, 2, at(beside, above), 8)
+        send(m, 2, 1, at(beside, above), to_below, in_sem.at[m, 13])
         share_shard(m, at(x, over))
-        for side in (below, above):
-            landed(m, 0, 1, at(beside, side))
-            landed(m, 3, 1, at(beside, side))
+        for side, index in ((below, 6), (above, 9)):
+            landed(m, 0, 1, at(beside, side), index)
+            landed(m, 3, 1, at(beside, side), index + 1)
             share_shard(m, at(beside, side))
 
     def fourth_round(m):
         for q in range(QUARTERS):
-            landed(m, q, 1, at(beside, over))
+            landed(m, q, 1, at(beside, over), 11 + q)
         share_shard(m, at(beside, over))
 
     def last_round(m):
-        for row in range(SIDE):
-            for chip in (x, beside):
-                landed(m, 0, 4, row * SIDE + jnp.where(native, SIDE - 1 - chip, chip))
+        wait_for(wall.at[m, :, pl.ds(0, 2 * SIDE)], share_in.at[m])
 
     def matrix(m, q):
         return wall[m, q].reshape(-1, quarter)
@@ -244,7 +240,7 @@
         wanted = plane * 2 + (group if c == 0 else 1 - group)
         return pltpu.make_async_remote_copy(
             src_ref=packed.at[q, wanted], dst_ref=arrived.at[q, ex],
-            send_sem=route_out.at[q, 2 * step + c], recv_sem=route_in.at[q, ex],
+            send_sem=route_out.at[q], recv_sem=route_in.at[q],
             device_id=device_at(x if c == 0 else partner, y, plane * 2 + group), device_id_type=MESH,
         )
 
@@ -252,7 +248,7 @@
         source = lax.rem(z + step, DEPTH) * 2 + (core if c == 0 else 1 - core)
         return pltpu.make_async_remote_copy(
             src_ref=results.at[q, source], dst_ref=returned.at[q, expert],
-            send_sem=back_out.at[q, 2 * step + c], recv_sem=back_in.at[q, expert],
+            send_sem=back_out.at[q], recv_sem=back_in.at[q],
             device_id=device_at(rows_x, y, source), device_id_type=MESH,
         )
 
@@ -272,42 +268,32 @@
         def _():
             make(q, 0, 0).start()
 
-    def scattered(make, q):
-        for step in far_first:
-            for c in (0, 1):
-                if step or c:
-                    make(q, step, c).wait_send()
+    def scattered(block, semaphore):
+        @pl.when(native)
+        def _():
+            wait_for(block.at[pl.ds(0, 15)], semaphore)
 
         @pl.when(jnp.logical_not(native))
         def _():
-            make(q, 0, 0).wait_send()
+            wait_for(block, semaphore)
+
+    def send_rows(q):
+        scatter(route_copy, q, pltpu.make_async_copy(packed.at[q, ex], arrived.at[q, ex], route_in.at[q]))
+
+    send_rows(0)
 
     @pl.when(native)
     def _():
         first_round(0)
         first_round(1)
 
-    key_copy.wait()
-    value_copy.wait()
-    kv_copies = []
-    copy = pltpu.make_async_remote_copy(
+    pltpu.make_async_remote_copy(
         src_ref=window.at[DEPTH, core], dst_ref=window.at[0, core],
         send_sem=kv_out.at[0], recv_sem=kv_in.at[0],
         device_id=(dp, next_ctx, ex), device_id_type=MESH,
-    )
-    copy.start()
-    kv_copies.append(copy)
-
-    hidden_copy.wait()
-    picks = slot_hits(routes[...]).reshape(count, -1).astype(jnp.bfloat16)
-    rows = hidden_rows[...].astype(jnp.float32)
-    scale = lax.rsqrt(jnp.mean(rows * rows, axis=-1, keepdims=True) + 1e-06)
-    for q in range(QUARTERS):
-        cols = pl.ds(q * quarter, quarter)
-        normed = (hidden_rows[:, cols].astype(jnp.float32) * scale * gain[:, cols]).astype(jnp.bfloat16)
-        block = jnp.dot(picks, normed, preferred_element_type=jnp.float32).astype(jnp.bfloat16)
-        packed[q] = block.reshape(16, CAP, quarter)
-        scatter(route_copy, q, pltpu.make_async_copy(packed.at[q, ex], arrived.at[q, ex], route_in.at[q, ex]))
+    ).start()
+    for q in range(1, QUARTERS):
+        send_rows(q)
 
     @pl.when(jnp.logical_not(native))
     def _():
@@ -326,22 +312,19 @@
     last_round(0)
     fourth_round(2)
     for q in range(QUARTERS):
-        scattered(route_copy, q)
-
-    pltpu.make_async_copy(window.at[0, core], window.at[0, core], kv_in.at[0]).wait()
+        scattered(packed.at[q], route_out.at[q])
+
+    wait_for(window.at[0, core], kv_in.at[0])
     for step in range(1, DEPTH):
         wraps = (z + step) // DEPTH
-        copy = pltpu.make_async_remote_copy(
+        pltpu.make_async_remote_copy(
             src_ref=window.at[DEPTH * (1 - wraps), core], dst_ref=window.at[DEPTH - step, core],
-            send_sem=kv_out.at[step], recv_sem=kv_in.at[DEPTH - step],
+            send_sem=kv_out.at[0], recv_sem=kv_in.at[1],
             device_id=(dp, ctx, lax.rem(z + step, DEPTH) * 2 + core), device_id_type=MESH,
-        )
-        copy.start()
-        kv_copies.append(copy)
-
-    for q in range(QUARTERS):
-        for source in range(16):
-            pltpu.make_async_copy(arrived.at[q, source], arrived.at[q, source], route_in.at[q, source]).wait()
+        ).start()
+
+    for q in range(QUARTERS):
+        wait_for(arrived.at[q], route_in.at[q])
     project(0)
     last_round(1)
     project(1)
@@ -352,24 +335,25 @@
     for q in range(QUARTERS):
         block = jnp.dot(active[...], matrix(2, q), preferred_element_type=jnp.float32)
         results[q] = block.astype(jnp.bfloat16).reshape(16, CAP, quarter)
-        scatter(back_copy, q, pltpu.make_async_copy(results.at[q, ex], returned.at[q, ex], back_in.at[q, ex]))
-
-    for slot in range(1, DEPTH):
-        pltpu.make_async_copy(window.at[slot, core], window.at[slot, core], kv_in.at[slot]).wait()
+        scatter(back_copy, q, pltpu.make_async_copy(results.at[q, ex], returned.at[q, ex], back_in.at[q]))
+
+    wait_for(window.at[pl.ds(1, DEPTH - 1), core], kv_in.at[1])
     share = pltpu.make_async_remote_copy(
         src_ref=window.at[:, core], dst_ref=window.at[:, core],
-        send_sem=kv_out.at[DEPTH], recv_sem=kv_in.at[DEPTH],
+        send_sem=kv_out.at[1], recv_sem=kv_in.at[2],
         device_id=to_sibling, device_id_type=MESH,
     )
     share.start()
     attention_bias(lengths, query_rows.shape[0], bias)
     query_copy.wait()
-    pltpu.make_async_copy(window.at[:, 1 - core], window.at[:, 1 - core], kv_in.at[DEPTH]).wait()
+    wait_for(window.at[:, 1 - core], kv_in.at[2])
 
     @pl.loop(0, QUERY_HEADS // HEADS_AT_ONCE)
     def _(i):
-        attend(i, query_rows, window, bias, context)
-
+        attend(i, query_rows, window, bias, context_rows)
+
+    context_copy = pltpu.make_async_copy(context_rows, context, local_sem.at[4])
+    context_copy.start()
     ids = lax.broadcasted_iota(jnp.int32, (16, routes.shape[1]), 0)
     weight = jnp.where(ids == routes[0:1, :], gates[0:1, :], 0.0)
     weight = weight + jnp.where(ids == routes[1:2, :], gates[1:2, :], 0.0)
@@ -377,27 +361,32 @@
     high = spread.astype(jnp.bfloat16)
     low = (spread - high.astype(jnp.float32)).astype(jnp.bfloat16)
     by_slot = (((0,), (0,)), ((), ()))
-    for q in range(QUARTERS):
-        for e in range(16):
-            pltpu.make_async_copy(returned.at[q, e], returned.at[q, e], back_in.at[q, e]).wait()
+    mixture_copies = []
+    for q in range(QUARTERS):
+        wait_for(returned.at[q], back_in.at[q])
         block = returned[q].reshape(count, quarter)
         total = lax.dot_general(high, block, by_slot, preferred_element_type=jnp.float32)
         total = total + lax.dot_general(low, block, by_slot, preferred_element_type=jnp.float32)
-        mixture[:, q * quarter:(q + 1) * quarter] = total.astype(mixture.dtype)
+        cols = pl.ds(q * quarter, quarter)
+        mixture_rows[:, cols] = total.astype(mixture.dtype)
+        copy = pltpu.make_async_copy(mixture_rows.at[:, cols], mixture.at[:, cols], local_sem.at[5 + q])
+        copy.start()
+        mixture_copies.append(copy)
 
     share.wait_send()
+    wait_for(window.at[pl.ds(0, DEPTH), core], kv_out.at[0])
     for m in range(3):
-        for copy in first_copies(m):
-            copy.wait_send()
-    for copy in kv_copies + sent:
-        copy.wait_send()
-    for q in range(QUARTERS):
-        scattered(back_copy, q)
+        wait_for(wall.at[m, :, pl.ds(0, 15)], out_sem.at[m])
+    for q in range(QUARTERS):
+        scattered(results.at[q], back_out.at[q])
 
     @pl.when(jnp.logical_not(native))
     def _():
-        for copy in shard_copies(True):
-            copy.wait_send()
+        wait_for(wall.at[:, :, y * SIDE + x], pass_out)
+
+    context_copy.wait()
+    for copy in mixture_copies:
+        copy.wait()
 
 
 def shards(queries, keys, values, lengths, hidden, norm_gain, routes, gates, w_gate, w_up, w_down):
@@ -412,10 +401,12 @@
         kernel,
         out_shape=(out, out),
         in_specs=[far] * 7 + [vmem] * 3 + [pl.BlockSpec(memory_space=pltpu.SMEM)],
-        out_specs=[vmem] * 2,
+        out_specs=[far] * 2,
         scratch_shapes=[
             pltpu.VMEM((3, QUARTERS, SIDE * SIDE, piece, quarter), bf16),
             pltpu.VMEM((DEPTH + 1, 2, tokens, 2 * keys.shape[1]), bf16),
+            pltpu.VMEM((tokens, width), bf16),
+            pltpu.VMEM((tokens, width), bf16),
             pltpu.VMEM((tokens, width), bf16),
             pltpu.VMEM((tokens, width), bf16),
             pltpu.VMEM((QUARTERS, 16, CAP, quarter), bf16),
@@ -425,8 +416,8 @@
             pltpu.VMEM((2, count, units), f32),
             pltpu.VMEM((count, units), bf16),
             pltpu.VMEM((tokens, (DEPTH + 1) * 2 * tokens), f32),
-            dma((4,)), dma((3, QUARTERS)), dma((3, 4)), dma((3, 20)), dma((3, 16, QUARTERS)), dma((QUARTERS, 16)), dma((QUARTERS, 16)),
-            dma((9,)), dma((9,)), dma((QUARTERS, 16)), dma((QUARTERS, 16)),
+            dma((9,)), dma(()), dma((3,)), dma((3,)), dma((3, 15)), dma((3,)), dma((QUARTERS,)), dma((QUARTERS,)),
+            dma((2,)), dma((3,)), dma((QUARTERS,)), dma((QUARTERS,)),
         ],
         compiler_params=pltpu.CompilerParams(
             collective_id=0, has_side_effects=True, vmem_limit_bytes=60 * 1024 * 1024

time: 184 us -> 178 us (0.967)
  Pallas kernels: 179 us -> 174 us
    pallas_call x1, Pallas kernels: 179 us -> 174 us  [shards(): pl.pallas_call(kernel, out_shape=(out, out), in_specs=[far] * 7 + [vmem]...]
where the time goes in v4:
time: 178 us
  Pallas kernels  174 us (98%)
  local copies, waits for them, and re-layouts  3.35 us (2%)
    pallas_call x1, Pallas kernels, shards(): pl.pallas_call(kernel, out_shape=(out, out), in_specs=[far] * 7 + [vmem]...  174 us

profile of v4, /device:TPU:1, one launch (start us, length us, event | category | flops | bytes accessed | tf_op | source)
XLA Modules:
  0.0 177.7 jit_solution(15265616547017943)
XLA Ops:
  0.6 173.7 %whole_block.1 = (bf16[128,4096]{1,0:T(8,128)(2,1)}, bf16[128,4096]{1,0:T(8,128)(2,1)}) custom-call(bf16[48,4096]{1,0:T(8,128)(2,1)} %bitcast.12, bf16[48,4096]{1,0:T(8,128)(2,1)} %bitcast.13, bf16[48,4096]{1,0:T(8,128)(2,1)} %bitcast.14, bf16[128,4096]{1,0:T(8,128)(2,1)} %queries.1, bf16[128,256]{1,0:T(8,128)(2,1)} %keys.1, bf16[128,256]{1,0:T(8,128)(2,1)} %values.1, ...), custom_call_target="tpu_custom_call" | custom-call | flops 20000000000 | bytes 10000000 | tf_op jit(solution)/shard_map/whole_block/pallas_call | solution.py:400
  174.4 0.0 copy-start
  174.4 2.4 %copy.15 = bf16[128,4096]{1,0:T(8,128)(2,1)} copy(bf16[128,4096]{1,0:T(8,128)(2,1)} %get-tuple-element.4) | data formatting | bytes 2097152
  176.7 0.0 copy-done
  176.7 1.0 copy.16
Async XLA Ops:
  174.4 2.4 %copy-start = (bf16[128,4096]{1,0:T(8,128)(2,1)S(1)}, bf16[128,4096]{1,0:T(8,128)(2,1)}, u32[]{:S(2)}) copy-start(bf16[128,4096]{1,0:T(8,128)(2,1)} %get-tuple-element.5) | copy-start | bytes 3145732

commit v5 on v4

--- a/solution.py
+++ b/solution.py
@@ -100,6 +100,8 @@
     sibling = z * 2 + 1 - core
     to_sibling = (dp, ctx, sibling)
     prior_ctx, next_ctx = lax.rem(ctx + 7, 8), lax.rem(ctx + 1, 8)
+    to_next = (dp, lax.rem(ctx + (z + 1) // DEPTH, 8), lax.rem(ex + 2, 16))
+    to_prior = (dp, lax.rem(ctx + 7 + (z + DEPTH - 1) // DEPTH, 8), lax.rem(ex + 14, 16))
     expert = z * 2 + group
     rows_x = jnp.where(native, x, partner)
     quarter = wall.shape[-1]
@@ -137,7 +139,7 @@
         copy.start()
 
     barrier = pltpu.get_barrier_semaphore()
-    for neighbour in (to_beside, to_above, to_below, (dp, prior_ctx, ex)):
+    for neighbour in (to_beside, to_above, to_below, (dp, prior_ctx, ex), to_next, to_prior):
         pl.semaphore_signal(barrier, inc=1, device_id=neighbour, device_id_type=MESH)
     for step in range(16):
         other = lax.rem(ex + step, 16)
@@ -156,7 +158,7 @@
         packed[q] = block.reshape(16, CAP, quarter)
     key_copy.wait()
     value_copy.wait()
-    pl.semaphore_wait(barrier, 4 + 15 + 16)
+    pl.semaphore_wait(barrier, 6 + 15 + 16)
 
     @pl.when(jnp.logical_not(native))
     def _():
@@ -280,6 +282,27 @@
     def send_rows(q):
         scatter(route_copy, q, pltpu.make_async_copy(packed.at[q, ex], arrived.at[q, ex], route_in.at[q]))
 
+    def pass_block(source, target, device, arrival):
+        pltpu.make_async_remote_copy(
+            src_ref=window.at[source, core], dst_ref=window.at[target, core],
+            send_sem=kv_out.at[0], recv_sem=kv_in.at[arrival],
+            device_id=device, device_id_type=MESH,
+        ).start()
+
+    def pass_blocks(hop):
+        if hop == 1:
+            wait_for(window.at[0, core], kv_in.at[0])
+        else:
+            wait_for(window.at[DEPTH + 1 - hop, core], kv_in.at[2 * hop - 3])
+            wait_for(window.at[hop - 1, core], kv_in.at[2 * hop - 2])
+        if hop < DEPTH // 2:
+            pass_block(DEPTH + 1 - hop, DEPTH - hop, to_next, 2 * hop - 1)
+            pass_block(hop - 1, hop, to_prior, 2 * hop)
+        else:
+            onwards = core == 0
+            device = tuple(jnp.where(onwards, a, b) for a, b in zip(to_next, to_prior))
+            pass_block(jnp.where(onwards, DEPTH // 2 + 1, DEPTH // 2 - 1), DEPTH // 2, device, DEPTH - 1)
+
     send_rows(0)
 
     @pl.when(native)
@@ -287,11 +310,7 @@
         first_round(0)
         first_round(1)
 
-    pltpu.make_async_remote_copy(
-        src_ref=window.at[DEPTH, core], dst_ref=window.at[0, core],
-        send_sem=kv_out.at[0], recv_sem=kv_in.at[0],
-        device_id=(dp, next_ctx, ex), device_id_type=MESH,
-    ).start()
+    pass_block(DEPTH, 0, (dp, next_ctx, ex), 0)
     for q in range(1, QUARTERS):
         send_rows(q)
 
@@ -307,29 +326,21 @@
     second_round(2)
     third_round(1)
     fourth_round(0)
+    pass_blocks(1)
     third_round(2)
     fourth_round(1)
     last_round(0)
-    fourth_round(2)
-    for q in range(QUARTERS):
-        scattered(packed.at[q], route_out.at[q])
-
-    wait_for(window.at[0, core], kv_in.at[0])
-    for step in range(1, DEPTH):
-        wraps = (z + step) // DEPTH
-        pltpu.make_async_remote_copy(
-            src_ref=window.at[DEPTH * (1 - wraps), core], dst_ref=window.at[DEPTH - step, core],
-            send_sem=kv_out.at[0], recv_sem=kv_in.at[1],
-            device_id=(dp, ctx, lax.rem(z + step, DEPTH) * 2 + core), device_id_type=MESH,
-        ).start()
-
+    pass_blocks(2)
     for q in range(QUARTERS):
         wait_for(arrived.at[q], route_in.at[q])
     project(0)
+    fourth_round(2)
+    pass_blocks(3)
     last_round(1)
     project(1)
     g = sums[0]
     active[...] = (g / (1.0 + jnp.exp(-g)) * sums[1]).astype(jnp.bfloat16)
+    pass_blocks(4)
     last_round(2)
 
     for q in range(QUARTERS):
@@ -337,16 +348,16 @@
         results[q] = block.astype(jnp.bfloat16).reshape(16, CAP, quarter)
         scatter(back_copy, q, pltpu.make_async_copy(results.at[q, ex], returned.at[q, ex], back_in.at[q]))
 
-    wait_for(window.at[pl.ds(1, DEPTH - 1), core], kv_in.at[1])
+    wait_for(window.at[DEPTH // 2, core], kv_in.at[DEPTH - 1])
     share = pltpu.make_async_remote_copy(
         src_ref=window.at[:, core], dst_ref=window.at[:, core],
-        send_sem=kv_out.at[1], recv_sem=kv_in.at[2],
+        send_sem=kv_out.at[1], recv_sem=kv_in.at[DEPTH],
         device_id=to_sibling, device_id_type=MESH,
     )
     share.start()
     attention_bias(lengths, query_rows.shape[0], bias)
     query_copy.wait()
-    wait_for(window.at[:, 1 - core], kv_in.at[2])
+    wait_for(window.at[:, 1 - core], kv_in.at[DEPTH])
 
     @pl.loop(0, QUERY_HEADS // HEADS_AT_ONCE)
     def _(i):
@@ -378,6 +389,7 @@
     for m in range(3):
         wait_for(wall.at[m, :, pl.ds(0, 15)], out_sem.at[m])
     for q in range(QUARTERS):
+        scattered(packed.at[q], route_out.at[q])
         scattered(results.at[q], back_out.at[q])
 
     @pl.when(jnp.logical_not(native))
@@ -417,7 +429,7 @@
             pltpu.VMEM((count, units), bf16),
             pltpu.VMEM((tokens, (DEPTH + 1) * 2 * tokens), f32),
             dma((9,)), dma(()), dma((3,)), dma((3,)), dma((3, 15)), dma((3,)), dma((QUARTERS,)), dma((QUARTERS,)),
-            dma((2,)), dma((3,)), dma((QUARTERS,)), dma((QUARTERS,)),
+            dma((2,)), dma((DEPTH + 1,)), dma((QUARTERS,)), dma((QUARTERS,)),
         ],
         compiler_params=pltpu.CompilerParams(
             collective_id=0, has_side_effects=True, vmem_limit_bytes=60 * 1024 * 1024

time: 178 us -> 174 us (0.978)
  Pallas kernels: 174 us -> 169 us
    pallas_call x1, Pallas kernels: 174 us -> 169 us  [shards(): pl.pallas_call(kernel, out_shape=(out, out), in_specs=[far] * 7 + [vmem]...]
where the time goes in v5:
time: 174 us; the launch traced here: 173 us
  Pallas kernels  169 us (97%)
  local copies, waits for them, and re-layouts  3.35 us (2%)
    pallas_call x1, Pallas kernels, shards(): pl.pallas_call(kernel, out_shape=(out, out), in_specs=[far] * 7 + [vmem]...  169 us

profile of v5, /device:TPU:1, one launch (start us, length us, event | category | flops | bytes accessed | tf_op | source)
XLA Modules:
  0.0 172.9 jit_solution(6523333078077588890)
XLA Ops:
  0.6 168.9 %whole_block.1 = (bf16[128,4096]{1,0:T(8,128)(2,1)}, bf16[128,4096]{1,0:T(8,128)(2,1)}) custom-call(bf16[48,4096]{1,0:T(8,128)(2,1)} %bitcast.12, bf16[48,4096]{1,0:T(8,128)(2,1)} %bitcast.13, bf16[48,4096]{1,0:T(8,128)(2,1)} %bitcast.14, bf16[128,4096]{1,0:T(8,128)(2,1)} %queries.1, bf16[128,256]{1,0:T(8,128)(2,1)} %keys.1, bf16[128,256]{1,0:T(8,128)(2,1)} %values.1, ...), custom_call_target="tpu_custom_call" | custom-call | flops 20000000000 | bytes 10000000 | tf_op jit(solution)/shard_map/whole_block/pallas_call | solution.py:412
  169.6 0.0 copy-start
  169.6 2.4 %copy.15 = bf16[128,4096]{1,0:T(8,128)(2,1)} copy(bf16[128,4096]{1,0:T(8,128)(2,1)} %get-tuple-element.4) | data formatting | bytes 2097152
  172.0 0.0 copy-done
  172.0 1.0 copy.16
Async XLA Ops:
  169.6 2.4 %copy-start = (bf16[128,4096]{1,0:T(8,128)(2,1)S(1)}, bf16[128,4096]{1,0:T(8,128)(2,1)}, u32[]{:S(2)}) copy-start(bf16[128,4096]{1,0:T(8,128)(2,1)} %get-tuple-element.5) | copy-start | bytes 3145732

commit v6 on v5

--- a/solution.py
+++ b/solution.py
@@ -282,12 +282,18 @@
     def send_rows(q):
         scatter(route_copy, q, pltpu.make_async_copy(packed.at[q, ex], arrived.at[q, ex], route_in.at[q]))
 
+    def wait_rows(q):
+        scattered(packed.at[q], route_out.at[q])
+
     def pass_block(source, target, device, arrival):
-        pltpu.make_async_remote_copy(
-            src_ref=window.at[source, core], dst_ref=window.at[target, core],
-            send_sem=kv_out.at[0], recv_sem=kv_in.at[arrival],
-            device_id=device, device_id_type=MESH,
-        ).start()
+        rows = window.shape[2] // 8
+        for part in range(8):
+            block = pl.ds(part * rows, rows)
+            pltpu.make_async_remote_copy(
+                src_ref=window.at[source, core, block], dst_ref=window.at[target, core, block],
+                send_sem=kv_out.at[0], recv_sem=kv_in.at[arrival],
+                device_id=device, device_id_type=MESH,
+            ).start()
 
     def pass_blocks(hop):
         if hop == 1:
@@ -311,8 +317,8 @@
         first_round(1)
 
     pass_block(DEPTH, 0, (dp, next_ctx, ex), 0)
-    for q in range(1, QUARTERS):
-        send_rows(q)
+    send_rows(1)
+    send_rows(2)
 
     @pl.when(jnp.logical_not(native))
     def _():
@@ -322,20 +328,22 @@
     second_round(0)
     first_round(2)
     second_round(1)
+    pass_blocks(1)
     third_round(0)
     second_round(2)
     third_round(1)
+    wait_rows(0)
+    send_rows(3)
     fourth_round(0)
-    pass_blocks(1)
     third_round(2)
     fourth_round(1)
+    pass_blocks(2)
     last_round(0)
-    pass_blocks(2)
     for q in range(QUARTERS):
         wait_for(arrived.at[q], route_in.at[q])
+    pass_blocks(3)
     project(0)
     fourth_round(2)
-    pass_blocks(3)
     last_round(1)
     project(1)
     g = sums[0]
@@ -389,7 +397,8 @@
     for m in range(3):
         wait_for(wall.at[m, :, pl.ds(0, 15)], out_sem.at[m])
     for q in range(QUARTERS):
-        scattered(packed.at[q], route_out.at[q])
+        if q >= 1:
+            scattered(packed.at[q], route_out.at[q])
         scattered(results.at[q], back_out.at[q])
 
     @pl.when(jnp.logical_not(native))

time: 174 us -> 172 us (0.989)
  Pallas kernels: 169 us -> 167 us
where the time goes in v6:
time: 172 us; the launch traced here: 171 us
  Pallas kernels  167 us (97%)
  local copies, waits for them, and re-layouts  3.35 us (2%)
    pallas_call x1, Pallas kernels, shards(): pl.pallas_call(kernel, out_shape=(out, out), in_specs=[far] * 7 + [vmem]...  167 us

profile of v6, /device:TPU:1, one launch (start us, length us, event | category | flops | bytes accessed | tf_op | source)
XLA Modules:
  0.0 171.4 jit_solution(11274378321565843862)
XLA Ops:
  0.6 167.4 %whole_block.1 = (bf16[128,4096]{1,0:T(8,128)(2,1)}, bf16[128,4096]{1,0:T(8,128)(2,1)}) custom-call(bf16[48,4096]{1,0:T(8,128)(2,1)} %bitcast.12, bf16[48,4096]{1,0:T(8,128)(2,1)} %bitcast.13, bf16[48,4096]{1,0:T(8,128)(2,1)} %bitcast.14, bf16[128,4096]{1,0:T(8,128)(2,1)} %queries.1, bf16[128,256]{1,0:T(8,128)(2,1)} %keys.1, bf16[128,256]{1,0:T(8,128)(2,1)} %values.1, ...), custom_call_target="tpu_custom_call" | custom-call | flops 20000000000 | bytes 10000000 | tf_op jit(solution)/shard_map/whole_block/pallas_call | solution.py:421
  168.0 0.0 copy-start
  168.0 2.4 %copy.15 = bf16[128,4096]{1,0:T(8,128)(2,1)} copy(bf16[128,4096]{1,0:T(8,128)(2,1)} %get-tuple-element.4) | data formatting | bytes 2097152
  170.4 0.0 copy-done
  170.4 1.0 copy.16
Async XLA Ops:
  168.0 2.4 %copy-start = (bf16[128,4096]{1,0:T(8,128)(2,1)S(1)}, bf16[128,4096]{1,0:T(8,128)(2,1)}, u32[]{:S(2)}) copy-start(bf16[128,4096]{1,0:T(8,128)(2,1)} %get-tuple-element.5) | copy-start | bytes 3145732
